TPU v7x, 128 devices: a whole 4x4x4 slice. The times are simulated.
128 devices in a mesh: probe: 4 (over z_lo, core), slab: 32 (over x, z_hi, y).
Axes of the slice: x: 4, y: 4, z: 4 (z_hi: 2, z_lo: 2; z = z_hi * 2 + z_lo), core: 2. Of those that a mesh axis runs over, the one named last changes fastest.
Arguments:
- probes: bfloat16 [8, 256, 256, 256], P('probe', 'slab'), may hold values from -3 to 3, as said below
- potential: float32 [256, 256, 256], P('slab'), may hold values from -0.4 to 0.4
- potential_change: float32 [256, 256, 256], P('slab'), may hold values from 0.2 to 1
- coefficients: float32 [3], replicated, may hold values from 0.5 to 1.5
Outputs:
- hartree_change: float32 [256, 256, 256], P('slab')
- moment_change: float32 [3], replicated
Inputs may be any that keep to these rules, and one draw needn't show every extreme that they name: `probes`: every entry of a probe vector is plus or minus one amplitude shared by that whole vector, at least 1.
All inputs are finite; a program needn't handle non-finite values.
Results may differ from a plain program's by a relative error of at most 0.00035.
Values may be sent and summed in bfloat16 or wider, within the bound.
A program may use at most 192 MiB of HBM per device.

v0:
```python
import math

import jax
import jax.numpy as jnp
from jax import lax
from jax.sharding import PartitionSpec as P

ORDER = 3


KINETIC = 1.0 / 12.0
CENTRE = 0.5
SCREEN = 0.05


def extended(block, sides, width):
    for axis, dim in sides:
        count = lax.axis_size(axis)
        forward = [(i, i + 1) for i in range(count - 1)]
        forward.append((count - 1, 0))
        backward = [(target, source) for source, target in forward]
        low = lax.ppermute(
            lax.slice_in_dim(block, block.shape[dim] - width, None, axis=dim), axis, forward
        )
        high = lax.ppermute(lax.slice_in_dim(block, 0, width, axis=dim), axis, backward)
        block = jnp.concatenate([low, block, high], axis=dim)
    return block


def hamiltonian(padded, potential):
    middle = padded[..., 1:-1, :, :]
    beside_all = padded[..., 2:, :, :] + padded[..., :-2, :, :]
    beside_all = beside_all + jnp.roll(middle, 1, -2) + jnp.roll(middle, -1, -2)
    beside_all = beside_all + jnp.roll(middle, 1, -1) + jnp.roll(middle, -1, -1)
    return KINETIC * (6.0 * middle - beside_all) + (potential - CENTRE) * middle


def signed_freq(first, count, size):
    values = first + jnp.arange(count, dtype=jnp.int32)
    return jnp.where(values <= size // 2, values, values - size)


def screened_kernel(planes, row_start, row_count, rows, cols):
    freq_z = signed_freq(0, planes, planes)
    freq_y = signed_freq(row_start, row_count, rows)
    freq_x = signed_freq(0, cols, cols)
    wave_z = (freq_z.astype(jnp.float32) * (2.0 * math.pi / planes)) ** 2
    wave_y = (freq_y.astype(jnp.float32) * (2.0 * math.pi / rows)) ** 2
    wave_x = (freq_x.astype(jnp.float32) * (2.0 * math.pi / cols)) ** 2
    summed = wave_z[:, None, None] + wave_y[None, :, None] + wave_x[None, None, :]
    values = 4.0 * math.pi / (summed + SCREEN * SCREEN)
    anchor = (
        (freq_z == 0)[:, None, None] & (freq_y == 0)[None, :, None] & (freq_x == 0)[None, None, :]
    )
    return jnp.where(anchor, 0.0, values)


def dft_tables(size, sign):
    values = jnp.arange(size, dtype=jnp.int32)
    phase = values[:, None] * values[None, :] % size
    angle = phase.astype(jnp.float32) * (2.0 * math.pi / size)
    return (jnp.cos(angle), sign * jnp.sin(angle))


def product(form, left, right):
    return jnp.einsum(form, left, right, precision=lax.Precision.HIGHEST)


def complex_apply(real_part, imag_part, tables, form):
    table_real, table_imag = tables
    new_real = product(form, real_part, table_real) - product(form, imag_part, table_imag)
    new_imag = product(form, real_part, table_imag) + product(form, imag_part, table_real)
    return (new_real, new_imag)


def forward_planes(field):
    table_real, table_imag = dft_tables(field.shape[2], -1.0)
    real_part = product("zyx,xk->zyk", field, table_real)
    imag_part = product("zyx,xk->zyk", field, table_imag)
    return complex_apply(real_part, imag_part, dft_tables(field.shape[1], -1.0), "zyx,yk->zkx")


def inverse_planes(real_part, imag_part, scale):
    real_part, imag_part = complex_apply(
        real_part, imag_part, dft_tables(real_part.shape[1], 1.0), "zyx,yk->zkx"
    )
    table_real, table_imag = dft_tables(real_part.shape[2], 1.0)
    result = product("zyx,xk->zyk", real_part, table_real) - product(
        "zyx,xk->zyk", imag_part, table_imag
    )
    return result * scale


def column_solve(real_part, imag_part, row_start, rows):
    planes = real_part.shape[0]
    real_part, imag_part = complex_apply(
        real_part, imag_part, dft_tables(planes, -1.0), "zyx,zk->kyx"
    )
    kernel = screened_kernel(planes, row_start, real_part.shape[1], rows, real_part.shape[2])
    real_part = real_part * kernel
    imag_part = imag_part * kernel
    return complex_apply(real_part, imag_part, dft_tables(planes, 1.0), "zyx,zk->kyx")


def per_device(probes, potential, potential_change, coefficients):
    panel, planes, rows, cols = probes.shape
    vector = probes.astype(jnp.float32)
    total_probes = panel * lax.axis_size("probe")
    grid_cells = planes * lax.axis_size("slab") * rows * cols

    def record(density, tallies, order_index, change):
        product_term = vector * change
        density = density + coefficients[order_index] * jnp.sum(product_term, axis=0)
        local_sum = jnp.sum(product_term)
        local_sum = lax.psum(local_sum, ("probe", "slab"))
        return (density, tallies + [local_sum])

    density = jnp.zeros((planes, rows, cols), jnp.float32)
    tallies = []
    padded = extended(probes, (("slab", 1),), 1).astype(jnp.float32)
    current = hamiltonian(padded, potential)
    current_change = potential_change * vector
    density, tallies = record(density, tallies, 0, current_change)
    earlier = vector
    earlier_change = jnp.zeros_like(vector)
    for order_index in range(1, ORDER):
        if order_index < ORDER - 1:
            stacked = jnp.stack([current, current_change])
            widened = extended(stacked, (("slab", 2),), 1)
            images = hamiltonian(widened, potential)
            following = 2.0 * images[0] - earlier
            following_change = 2.0 * (images[1] + potential_change * current)
        else:
            widened = extended(current_change, (("slab", 1),), 1)
            following = current
            following_change = (
                2.0 * (hamiltonian(widened, potential) + potential_change * current)
                - earlier_change
            )
        density, tallies = record(density, tallies, order_index, following_change)
        earlier, earlier_change = (current, current_change)
        current, current_change = (following, following_change)
    moments = jnp.stack(tallies)
    moment_change = moments / (total_probes * grid_cells)
    density = density / total_probes
    scale = 1.0 / grid_cells
    summed = lax.psum(density, "probe")
    real_part, imag_part = forward_planes(summed)
    real_part, imag_part = (
        lax.all_to_all(real_part, "slab", split_axis=1, concat_axis=0, tiled=True),
        lax.all_to_all(imag_part, "slab", split_axis=1, concat_axis=0, tiled=True),
    )
    row_start = lax.axis_index("slab") * real_part.shape[1]
    real_part, imag_part = column_solve(real_part, imag_part, row_start, rows)
    real_part, imag_part = (
        lax.all_to_all(real_part, "slab", split_axis=0, concat_axis=1, tiled=True),
        lax.all_to_all(imag_part, "slab", split_axis=0, concat_axis=1, tiled=True),
    )
    hartree_change = inverse_planes(real_part, imag_part, scale)
    return (hartree_change, moment_change)


def solution(mesh):
    return jax.shard_map(
        per_device,
        mesh=mesh,
        in_specs=(
            P("probe", "slab", None, None),
            P("slab", None, None),
            P("slab", None, None),
            P(),
        ),
        out_specs=(P("slab", None, None), P()),
        check_vma=False,
    )
```

profile of v0, /device:TPU:1, one launch (start us, length us, event | category | flops | bytes accessed | tf_op | source)
XLA Modules:
  0.0 484.7 jit_solution(14794644724971652452)
XLA Ops:
  10.5 7.0 %collective-permute-start.1 = (bf16[2,1,256,256]{3,2,1,0:T(8,128)(2,1)S(1)}, bf16[2,1,256,256]{3,2,1,0:T(8,128)(2,1)S(1)}, u32[]{:S(2)}, u32[]{:S(2)}) collective-permute-start(bf16[2,1,256,256]{3,2,1,0:T(8,128)(2,1)S(1)} %get-tuple-element.45), channel_id=1, source_target_pairs={{1,0},{2,1},{3,2},{4,3},{5,4},{6,5},{7,6},{8,7},{9,8},{10,9},{11,1... | collective-permute-start | bytes 786440 | tf_op jit(solution)/shard_map/ppermute | solution.py:25
  17.5 4.6 fusion.13
  25.6 4.8 fusion.231
  37.3 9.2 %fusion.37 = f32[2,8,256,256]{3,2,1,0:T(8,128)S(1)} fusion(f32[2,10,256,256]{3,2,1,0:T(8,128)S(1)} %maximum_convert_fusion, f32[2,8,255,256]{3,2,1,0:T(8,128)} %get-tuple-element.29, f32[2,8,1,256]{3,2,1,0:T(1,128)S(1)} %get-tuple-element.41, f32[2,8,1,256]{3,2,1,0:T(1,128)S(1)} %get-tuple-element.40, f32[2,8,255,256]{3,2,1,0:T(8,128)} %get-tuple-element.28, ...), kind=kLoop, calls=%fused_computation.72 | loop fusion | flops 14680064 | bytes 35651584 | tf_op jit(solution)/shard_map/add | solution.py:35
  46.5 7.2 %fusion.20 = (f32[2,2,8,256,1]{4,3,2,1,0:T(8,128)}, f32[2,2,8,256,1]{4,3,2,1,0:T(8,128)}) fusion(f32[1,2,8,256,256]{4,3,2,1,0:T(8,128)S(1)} %bitcast.139, f32[1,2,8,256,256]{4,3,2,1,0:T(8,128)} %fusion.13), kind=kLoop, calls=%fused_computation.50 | loop fusion | flops 16384 | bytes 8454144 | tf_op jit(solution)/shard_map/stack | solution.py:128
  53.9 5.3 %collective-permute-start.2 = (f32[2,2,1,256,256]{4,3,2,1,0:T(8,128)S(1)}, f32[2,2,1,256,256]{4,3,2,1,0:T(8,128)S(1)}, u32[]{:S(2)}, u32[]{:S(2)}) collective-permute-start(f32[2,2,1,256,256]{4,3,2,1,0:T(8,128)S(1)} %get-tuple-element.22), channel_id=1, source_target_pairs={{1,0},{2,1},{3,2},{4,3},{5,4},{6,5},{7,6},{8,7},{9,8},{10,9},{11,1... | collective-permute-start | bytes 3145736 | tf_op jit(solution)/shard_map/ppermute | solution.py:25
  59.4 7.6 %fusion.3 = (f32[2,2,8,256,255]{4,3,2,1,0:T(8,128)}, f32[2,2,8,256,255]{4,3,2,1,0:T(8,128)}) fusion(f32[1,2,8,256,256]{4,3,2,1,0:T(8,128)S(1)} %bitcast.142, f32[1,2,8,256,256]{4,3,2,1,0:T(8,128)S(1)} %copy-done.2), kind=kLoop, calls=%fused_computation.24 | loop fusion | flops 4177920 | bytes 25100288 | tf_op jit(solution)/shard_map/stack | solution.py:128
  67.0 6.7 %fusion.1 = (f32[2,2,8,255,256]{4,3,2,1,0:T(8,128)}, f32[2,2,8,255,256]{4,3,2,1,0:T(8,128)}) fusion(f32[1,2,8,256,256]{4,3,2,1,0:T(8,128)S(1)} %bitcast.143, f32[1,2,8,256,256]{4,3,2,1,0:T(8,128)S(1)} %copy-done.2), kind=kLoop, calls=%fused_computation.22 | loop fusion | flops 4177920 | bytes 25100288 | tf_op jit(solution)/shard_map/stack | solution.py:128
  73.7 6.4 %collective-permute-done.2 = f32[2,2,1,256,256]{4,3,2,1,0:T(8,128)S(1)} collective-permute-done((f32[2,2,1,256,256]{4,3,2,1,0:T(8,128)S(1)}, f32[2,2,1,256,256]{4,3,2,1,0:T(8,128)S(1)}, u32[]{:S(2)}, u32[]{:S(2)}) %collective-permute-start.2) | collective-permute-done | bytes 1048608 | tf_op jit(solution)/shard_map/ppermute | solution.py:25
  80.1 7.8 %collective-permute-done.3 = f32[2,2,1,256,256]{4,3,2,1,0:T(8,128)S(1)} collective-permute-done((f32[2,2,1,256,256]{4,3,2,1,0:T(8,128)S(1)}, f32[2,2,1,256,256]{4,3,2,1,0:T(8,128)S(1)}, u32[]{:S(2)}, u32[]{:S(2)}) %collective-permute-start.3) | collective-permute-done | bytes 1048608 | tf_op jit(solution)/shard_map/ppermute | solution.py:22
  87.9 19.4 %fusion.11 = f32[2,2,8,256,256]{4,3,2,1,0:T(8,128)} fusion(f32[2,2,1,256,256]{4,3,2,1,0:T(8,128)S(1)} %collective-permute-done.3, f32[1,2,8,256,256]{4,3,2,1,0:T(8,128)S(1)} %copy-done.2, f32[1,2,8,256,256]{4,3,2,1,0:T(8,128)S(1)} %bitcast.144, f32[2,2,1,256,256]{4,3,2,1,0:T(8,128)S(1)} %collective-permute-done.2, ...), kind=kLoop, calls=%fused_computation.33 | loop fusion | flops 39845888 | bytes 54525952 | tf_op jit(solution)/shard_map/add | solution.py:35
  107.4 6.3 %fusion.14 = (f32[]{:T(128)}, f32[8,256,256]{2,1,0:T(8,128)}, f32[8,256,256]{2,1,0:T(8,128)}, f32[]{:T(128)}, f32[2,8,256,256]{3,2,1,0:T(8,128)S(1)}) fusion(bf16[2,8,256,256]{3,2,1,0:T(8,128)(2,1)S(1)} %copy-done.3, f32[8,256,256]{2,1,0:T(8,128)} %param.6, f32[2,8,256,256]{3,2,1,0:T(8,128)S(1)} %fusion.37, f32[2,2,8,256,256]{4,3,2,1,0:T(8,128)} %fusion.11), kind=kLoop, calls=%fused_computation.44 | loop fusion | flops 10485758 | bytes 20971528 | tf_op jit(solution)/shard_map/reduce_sum | solution.py:114
  113.7 4.8 fusion.234
  127.0 5.1 %collective-permute-done.4 = f32[2,1,256,256]{3,2,1,0:T(8,128)S(1)} collective-permute-done((f32[2,1,256,256]{3,2,1,0:T(8,128)S(1)}, f32[2,1,256,256]{3,2,1,0:T(8,128)S(1)}, u32[]{:S(2)}, u32[]{:S(2)}) %collective-permute-start.4) | collective-permute-done | bytes 524320 | tf_op jit(solution)/shard_map/ppermute | solution.py:25
  132.1 5.9 %collective-permute-done.5 = f32[2,1,256,256]{3,2,1,0:T(8,128)S(1)} collective-permute-done((f32[2,1,256,256]{3,2,1,0:T(8,128)S(1)}, f32[2,1,256,256]{3,2,1,0:T(8,128)S(1)}, u32[]{:S(2)}, u32[]{:S(2)}) %collective-permute-start.5) | collective-permute-done | bytes 524320 | tf_op jit(solution)/shard_map/ppermute | solution.py:22
  137.9 19.0 %fusion.230 = (f32[]{:T(128)}, f32[8,256,256]{2,1,0:T(8,128)}) fusion(f32[2,2,8,256,256]{4,3,2,1,0:T(8,128)} %fusion.11, f32[8,256,256]{2,1,0:T(8,128)} %get-tuple-element.42, f32[2,8,256,1]{3,2,1,0:T(8,128)} %get-tuple-element.32, f32[2,8,256,255]{3,2,1,0:T(8,128)} %get-tuple-element.30, f32[2,8,256,255]{3,2,1,0:T(8,128)} %get-tuple-element.31, ...), kind=kLoop, calls=%fused_computation.265 | loop fusion | flops 29884416 | bytes 42991620 | tf_op jit(solution)/shard_map/reduce_sum | solution.py:114
  156.9 6.4 %add_multiply_fusion.1 = f32[8,256,256]{2,1,0:T(8,128)} fusion(f32[8,256,256]{2,1,0:T(8,128)} %get-tuple-element.7, f32[8,256,256]{2,1,0:T(8,128)} %get-tuple-element.8, f32[8,256,256]{2,1,0:T(8,128)} %get-tuple-element.5, f32[]{:T(128)} %bitcast.9, f32[]{:T(128)} %bitcast.5, f32[]{:T(128)} %bitcast.4), kind=kLoop, calls=%fused_computation.104 | loop fusion | flops 3145728 | bytes 8388620 | tf_op jit(solution)/shard_map/div | solution.py:145
  163.3 55.2 %all-reduce.3.cloned.1.call-done = f32[8,256,256]{2,1,0:T(8,128)} async-done(((f32[8,256,256]{2,1,0:T(8,128)}), f32[8,256,256]{2,1,0:T(8,128)}) %all-reduce.3.cloned.1.call-update) | async-done | bytes 2097168 | tf_op jit(solution)/shard_map/psum | solution.py:147
  218.6 4.6 fusion.99
  236.0 9.2 %all-to-all-start.1 = ((f32[8,256,256]{2,0,1:T(8,128)}), f32[8,256,256]{2,0,1:T(8,128)}, u32[]{:S(2)}, u32[]{:S(2)}) async-start(f32[8,256,256]{2,0,1:T(8,128)} %copy.65), calls=%async_computation.1 | async-start | bytes 4194304 | tf_op jit(solution)/shard_map/all_to_all | solution.py:151
  255.1 18.9 %all-to-all-done.1 = f32[8,256,256]{2,0,1:T(8,128)} async-done(((f32[8,256,256]{2,0,1:T(8,128)}), f32[8,256,256]{2,0,1:T(8,128)}, u32[]{:S(2)}, u32[]{:S(2)}) %all-to-all-start.1) | async-done | bytes 2097184 | tf_op jit(solution)/shard_map/all_to_all | solution.py:151
  274.0 6.1 %all-to-all-start = ((f32[8,256,256]{2,0,1:T(8,128)}), f32[8,256,256]{2,0,1:T(8,128)S(1)}, u32[]{:S(2)}, u32[]{:S(2)}) async-start(f32[8,256,256]{2,0,1:T(8,128)} %copy.60), calls=%async_computation | async-start | bytes 4194304 | tf_op jit(solution)/shard_map/all_to_all | solution.py:150
  280.4 5.8 %fusion.52 = f32[256,8,256]{2,0,1:T(8,128)} fusion(f32[8,32,8,256]{3,0,2,1:T(8,128)} %bitcast.22), kind=kOutput, calls=%fused_computation.88 | convolution fusion | flops 1611530240 | bytes 4194304 | tf_op jit(solution)/shard_map/zyx,zk->kyx/dot_general | solution.py:66
  286.2 5.8 %fusion.54 = f32[256,8,256]{2,0,1:T(8,128)} fusion(f32[8,32,8,256]{3,0,2,1:T(8,128)} %bitcast.22), kind=kOutput, calls=%fused_computation.90 | convolution fusion | flops 1611595776 | bytes 4194304 | tf_op jit(solution)/shard_map/zyx,zk->kyx/dot_general | solution.py:66
  291.9 16.0 %all-to-all-done = f32[8,256,256]{2,0,1:T(8,128)S(1)} async-done(((f32[8,256,256]{2,0,1:T(8,128)}), f32[8,256,256]{2,0,1:T(8,128)S(1)}, u32[]{:S(2)}, u32[]{:S(2)}) %all-to-all-start) | async-done | bytes 2097184 | tf_op jit(solution)/shard_map/all_to_all | solution.py:150
  307.9 5.2 %add_multiply_fusion = f32[256,8,256]{2,0,1:T(8,128)S(1)} fusion(f32[256,8,256]{2,0,1:T(8,128)} %fusion.52, f32[8,32,8,256]{3,0,2,1:T(8,128)S(1)} %bitcast.147, f32[256]{0:T(256)S(1)} %multiply_multiply_fusion, f32[256,8]{0,1:T(8,128)S(1)} %broadcast_add_fusion.1, pred[256]{0:T(512)(128)(4,1)S(1)} %fusion.144, pred[256,8]{0,1:T(8,128)(4,1)S(1)} %broadcast_and_fusion), kind=kOutput, calls=%fused_computation.99 | convolution fusion | flops 1615265792 | bytes 6302976 | tf_op jit(solution)/shard_map/zyx,zk->kyx/dot_general | solution.py:66
  326.4 7.0 %all-to-all-start.3 = ((f32[256,8,256]{2,1,0:T(8,128)}), f32[256,8,256]{2,1,0:T(8,128)S(1)}, u32[]{:S(2)}, u32[]{:S(2)}) async-start(f32[256,8,256]{2,1,0:T(8,128)} %copy.77), calls=%async_computation.3 | async-start | bytes 4194304 | tf_op jit(solution)/shard_map/all_to_all | solution.py:157
  333.3 4.6 fusion.104
  343.4 18.1 %all-to-all-done.3 = f32[256,8,256]{2,1,0:T(8,128)S(1)} async-done(((f32[256,8,256]{2,1,0:T(8,128)}), f32[256,8,256]{2,1,0:T(8,128)S(1)}, u32[]{:S(2)}, u32[]{:S(2)}) %all-to-all-start.3) | async-done | bytes 2097184 | tf_op jit(solution)/shard_map/all_to_all | solution.py:157
  361.5 6.2 %all-to-all-start.2 = ((f32[256,8,256]{2,1,0:T(8,128)}), f32[256,8,256]{2,1,0:T(8,128)}, u32[]{:S(2)}, u32[]{:S(2)}) async-start(f32[256,8,256]{2,1,0:T(8,128)} %copy.72), calls=%async_computation.2 | async-start | bytes 4194304 | tf_op jit(solution)/shard_map/all_to_all | solution.py:156
  367.7 82.8 %all-reduce = (f32[1]{0:T(128)}, f32[1]{0:T(128)}, f32[1]{0:T(128)}) all-reduce(f32[1]{0:T(128)} %bitcast.46, f32[1]{0:T(128)} %bitcast.45, f32[1]{0:T(128)} %bitcast.44), channel_id=1, replica_groups=mesh['probe'=4,'slab'=32] {'probe','slab'}, use_global_device_ids=true, to_apply=%region_9.10 | all-reduce | flops 3 | bytes 24 | tf_op jit(solution)/shard_map/psum | solution.py:115
  461.3 4.6 fusion.48
  (75 shorter events, 86.4 us)
Async XLA Ops:
  7.2 211.4 %all-reduce.3.cloned.1.call-start = ((), (), s32[]{:S(2)}) async-start(), calls=%async_computation.4 | async-start | bytes 4194304 | tf_op jit(solution)/shard_map/psum | solution.py:147
  8.3 16.9 %collective-permute-start = (bf16[2,1,256,256]{3,2,1,0:T(8,128)(2,1)S(1)}, bf16[2,1,256,256]{3,2,1,0:T(8,128)(2,1)S(1)}, u32[]{:S(2)}, u32[]{:S(2)}) collective-permute-start(bf16[2,1,256,256]{3,2,1,0:T(8,128)(2,1)S(1)} %get-tuple-element.44), channel_id=1, source_target_pairs={{0,1},{1,2},{2,3},{3,4},{4,5},{5,6},{6,7},{7,8},{8,9},{9,10},{10,1... | collective-permute-start | bytes 786440 | tf_op jit(solution)/shard_map/ppermute | solution.py:22
  10.5 11.7 %copy-start.13 = (f32[3]{0:T(128)S(1)}, f32[3]{0:T(128)}, u32[]{:S(2)}) copy-start(f32[3]{0:T(128)} %param.7) | copy-start | bytes 40
  10.5 12.3 %copy-start.11 = (f32[8,256,256]{2,1,0:T(8,128)S(1)}, f32[8,256,256]{2,1,0:T(8,128)}, u32[]{:S(2)}) copy-start(f32[8,256,256]{2,1,0:T(8,128)} %param.5) | copy-start | bytes 6291460
  10.5 14.7 %collective-permute-start.1 = (bf16[2,1,256,256]{3,2,1,0:T(8,128)(2,1)S(1)}, bf16[2,1,256,256]{3,2,1,0:T(8,128)(2,1)S(1)}, u32[]{:S(2)}, u32[]{:S(2)}) collective-permute-start(bf16[2,1,256,256]{3,2,1,0:T(8,128)(2,1)S(1)} %get-tuple-element.45), channel_id=1, source_target_pairs={{1,0},{2,1},{3,2},{4,3},{5,4},{6,5},{7,6},{8,7},{9,8},{10,9},{11,1... | collective-permute-start | bytes 786440 | tf_op jit(solution)/shard_map/ppermute | solution.py:25
  22.1 3.1 copy-start.3
  46.5 60.9 %copy-start = (f32[2,8,256,256]{3,2,1,0:T(8,128)}, f32[2,8,256,256]{3,2,1,0:T(8,128)S(1)}, u32[]{:S(2)}) copy-start(f32[2,8,256,256]{3,2,1,0:T(8,128)S(1)} %fusion.37) | copy-start | bytes 12582916
  46.5 7.2 %copy-start.2 = (f32[1,2,8,256,256]{4,3,2,1,0:T(8,128)S(1)}, f32[1,2,8,256,256]{4,3,2,1,0:T(8,128)}, u32[]{:S(2)}) copy-start(f32[1,2,8,256,256]{4,3,2,1,0:T(8,128)} %fusion.13) | copy-start | bytes 12582916
  53.9 26.2 %collective-permute-start.2 = (f32[2,2,1,256,256]{4,3,2,1,0:T(8,128)S(1)}, f32[2,2,1,256,256]{4,3,2,1,0:T(8,128)S(1)}, u32[]{:S(2)}, u32[]{:S(2)}) collective-permute-start(f32[2,2,1,256,256]{4,3,2,1,0:T(8,128)S(1)} %get-tuple-element.22), channel_id=1, source_target_pairs={{1,0},{2,1},{3,2},{4,3},{5,4},{6,5},{7,6},{8,7},{9,8},{10,9},{11,1... | collective-permute-start | bytes 3145736 | tf_op jit(solution)/shard_map/ppermute | solution.py:25
  59.2 28.7 %collective-permute-start.3 = (f32[2,2,1,256,256]{4,3,2,1,0:T(8,128)S(1)}, f32[2,2,1,256,256]{4,3,2,1,0:T(8,128)S(1)}, u32[]{:S(2)}, u32[]{:S(2)}) collective-permute-start(f32[2,2,1,256,256]{4,3,2,1,0:T(8,128)S(1)} %get-tuple-element.23), channel_id=1, source_target_pairs={{0,1},{1,2},{2,3},{3,4},{4,5},{5,6},{6,7},{7,8},{8,9},{9,10},{10,1... | collective-permute-start | bytes 3145736 | tf_op jit(solution)/shard_map/ppermute | solution.py:22
  113.7 9.2 %copy-start.1 = (f32[2,8,256,256]{3,2,1,0:T(8,128)}, f32[2,8,256,256]{3,2,1,0:T(8,128)S(1)}, u32[]{:S(2)}) copy-start(f32[2,8,256,256]{3,2,1,0:T(8,128)S(1)} %get-tuple-element.13) | copy-start | bytes 12582916
  121.3 10.7 %collective-permute-start.4 = (f32[2,1,256,256]{3,2,1,0:T(8,128)S(1)}, f32[2,1,256,256]{3,2,1,0:T(8,128)S(1)}, u32[]{:S(2)}, u32[]{:S(2)}) collective-permute-start(f32[2,1,256,256]{3,2,1,0:T(8,128)S(1)} %get-tuple-element.38), channel_id=1, source_target_pairs={{1,0},{2,1},{3,2},{4,3},{5,4},{6,5},{7,6},{8,7},{9,8},{10,9},{11,1... | collective-permute-start | bytes 1572872 | tf_op jit(solution)/shard_map/ppermute | solution.py:25
  121.5 16.4 %collective-permute-start.5 = (f32[2,1,256,256]{3,2,1,0:T(8,128)S(1)}, f32[2,1,256,256]{3,2,1,0:T(8,128)S(1)}, u32[]{:S(2)}, u32[]{:S(2)}) collective-permute-start(f32[2,1,256,256]{3,2,1,0:T(8,128)S(1)} %get-tuple-element.39), channel_id=1, source_target_pairs={{0,1},{1,2},{2,3},{3,4},{4,5},{5,6},{6,7},{7,8},{8,9},{9,10},{10,1... | collective-permute-start | bytes 1572872 | tf_op jit(solution)/shard_map/ppermute | solution.py:22
  218.5 8.8 %copy-start.9 = (f32[8,256,256]{2,1,0:T(8,128)S(1)}, f32[8,256,256]{2,1,0:T(8,128)}, u32[]{:S(2)}) copy-start(f32[8,256,256]{2,1,0:T(8,128)} %all-reduce.3.cloned.1.call-done) | copy-start | bytes 6291460
  223.1 1.3 copy-start.4
  236.0 38.1 %all-to-all-start.1 = ((f32[8,256,256]{2,0,1:T(8,128)}), f32[8,256,256]{2,0,1:T(8,128)}, u32[]{:S(2)}, u32[]{:S(2)}) async-start(f32[8,256,256]{2,0,1:T(8,128)} %copy.65), calls=%async_computation.1 | async-start | bytes 4194304 | tf_op jit(solution)/shard_map/all_to_all | solution.py:151
  274.0 33.9 %all-to-all-start = ((f32[8,256,256]{2,0,1:T(8,128)}), f32[8,256,256]{2,0,1:T(8,128)S(1)}, u32[]{:S(2)}, u32[]{:S(2)}) async-start(f32[8,256,256]{2,0,1:T(8,128)} %copy.60), calls=%async_computation | async-start | bytes 4194304 | tf_op jit(solution)/shard_map/all_to_all | solution.py:150
  307.9 5.2 %copy-start.12 = (f32[256,8,256]{2,0,1:T(8,128)S(1)}, f32[256,8,256]{2,0,1:T(8,128)}, u32[]{:S(2)}) copy-start(f32[256,8,256]{2,0,1:T(8,128)} %fusion.54) | copy-start | bytes 6291460
  313.1 7.8 %copy-start.5 = (f32[256,8,256]{2,0,1:T(8,128)}, f32[256,8,256]{2,0,1:T(8,128)S(1)}, u32[]{:S(2)}) copy-start(f32[256,8,256]{2,0,1:T(8,128)S(1)} %add_multiply_fusion) | copy-start | bytes 6291460
  316.8 1.3 copy-start.8
  326.4 35.1 %all-to-all-start.3 = ((f32[256,8,256]{2,1,0:T(8,128)}), f32[256,8,256]{2,1,0:T(8,128)S(1)}, u32[]{:S(2)}, u32[]{:S(2)}) async-start(f32[256,8,256]{2,1,0:T(8,128)} %copy.77), calls=%async_computation.3 | async-start | bytes 4194304 | tf_op jit(solution)/shard_map/all_to_all | solution.py:157
  333.3 4.6 copy-start.6
  361.5 99.8 %all-to-all-start.2 = ((f32[256,8,256]{2,1,0:T(8,128)}), f32[256,8,256]{2,1,0:T(8,128)}, u32[]{:S(2)}, u32[]{:S(2)}) async-start(f32[256,8,256]{2,1,0:T(8,128)} %copy.72), calls=%async_computation.2 | async-start | bytes 4194304 | tf_op jit(solution)/shard_map/all_to_all | solution.py:156
  461.3 9.1 %copy-start.7 = (f32[256,8,256]{2,0,1:T(8,128)S(1)}, f32[256,8,256]{2,0,1:T(8,128)}, u32[]{:S(2)}) copy-start(f32[256,8,256]{2,0,1:T(8,128)} %fusion.44) | copy-start | bytes 6291460
  470.4 3.1 copy-start.10
Sparse Core Ops, SparseCore 0:
  163.5 55.0 all-reduce.2
where the time goes:
time: 491 us; the launch traced here: 485 us
  waiting for transfers between devices  133 us (27%)
  other arithmetic  92.1 us (19%)
  blocking collectives  82.8 us (17%)
  matrix products  79.1 us (16%)
  starting transfers between devices  44.8 us (9%)
  local copies, waits for them, and re-layouts  37.8 us (8%)
  between operations  14.6 us (3%)
    psum x1, blocking collectives, record(): local_sum = lax.psum(local_sum, ('probe', 'slab'))  82.8 us
    dot_general x20, matrix products, product(): return jnp.einsum(form, left, right, precision=lax.Precision.HIGHEST)  79.1 us
    psum x1, waiting for transfers between devices, per_device(): summed = lax.psum(density, 'probe')  55.2 us
    add x2, other arithmetic, hamiltonian(): return KINETIC * (6.0 * middle - beside_all) + (potential - CENTRE) * middle  28.7 us
    another operation x6, other arithmetic, per_device(): stacked = jnp.stack([current, current_change])  26.4 us
    reduce_sum x2, other arithmetic, record(): local_sum = jnp.sum(product_term)  25.2 us
    all_to_all x1, waiting for transfers between devices, per_device(): lax.all_to_all(imag_part, 'slab', split_axis=1, concat_axis=0, tiled=True)  18.9 us
    all_to_all x1, waiting for transfers between devices, per_device(): lax.all_to_all(imag_part, 'slab', split_axis=0, concat_axis=1, tiled=True)  18.1 us
  transfers between devices with their start and end apart: 11, of which 8 were waited for; matrix products, arithmetic and copies ran while one was open for 14% of the time, Pallas kernels for 0%

commit v1 on v0

v1 whole, which is shorter than its diff:
```python
import functools
import math

import jax
import jax.numpy as jnp
import ml_dtypes
import numpy as np
from jax import lax
from jax.experimental import pallas as pl
from jax.experimental.pallas import tpu as pltpu
from jax.sharding import PartitionSpec as P

MESH = pl.DeviceIdType.MESH
F32 = jnp.float32
BF16 = jnp.bfloat16
KINETIC = 1.0 / 12.0
SCREEN = 0.05
CHUNK = 256
PAD = 8


def cas_split(size):
    index = np.arange(size)
    angle = (index[:, None] * index[None, :] % size) * (2.0 * np.pi / size)
    table = np.cos(angle) + np.sin(angle)
    high = table.astype(ml_dtypes.bfloat16)
    low = (table - high.astype(np.float64)).astype(ml_dtypes.bfloat16)
    return high, low


def shuffle(size):
    index = np.arange(size)
    return index % 8 * (size // 8) + index // 8


def tables(*pairs):
    return jnp.asarray(np.stack([part for pair in pairs for part in pair]))


def split(value):
    high = value.astype(BF16)
    low = (value - high.astype(F32)).astype(BF16)
    return high, low


def times_table(value, table):
    high, low = split(value)
    total = jnp.dot(high, table[0], preferred_element_type=F32)
    total = total + jnp.dot(high, table[1], preferred_element_type=F32)
    return total + jnp.dot(low, table[0], preferred_element_type=F32)


def table_times(table, value):
    high, low = split(value)
    total = jnp.dot(table[0], high, preferred_element_type=F32)
    total = total + jnp.dot(table[1], high, preferred_element_type=F32)
    return total + jnp.dot(table[0], low, preferred_element_type=F32)


def place():
    probe = lax.axis_index("probe")
    slab = lax.axis_index("slab")
    return probe, slab


def sibling_of(probe, slab):
    return {"probe": probe + 1 - 2 * lax.rem(probe, 2), "slab": slab}


def partner_of(probe, slab):
    return {"probe": lax.rem(probe + 2, 4), "slab": slab}


def greet(peers):
    barrier = pltpu.get_barrier_semaphore()
    for peer in peers:
        pl.semaphore_signal(barrier, inc=1, device_id=peer, device_id_type=MESH)
    pl.semaphore_wait(barrier, len(peers))


def remote(source, target, sems, index, peer):
    return pltpu.make_async_remote_copy(
        src_ref=source,
        dst_ref=target,
        send_sem=sems[0].at[index],
        recv_sem=sems[1].at[index],
        device_id=peer,
        device_id_type=MESH,
    )


def density_kernel(
    slabs,
    coef_ref, table_ref, probes_ref, pot_ref, change_ref,
    out_ref, moment_ref,
    tab, v16, pot, change, near, weight, v32, qbuf, tbuf, ubuf, dbuf, ybuf, rone, rtwo, mbuf,
    load_sems, halo_s, halo_r, fwd_s, fwd_r, one_s, one_r, two_s, two_r, mom_s, mom_r,
):
    probe, slab = place()
    core = lax.rem(probe, 2)
    zlow = probe // 2
    above = {"probe": probe, "slab": lax.rem(slab + 1, slabs)}
    below = {"probe": probe, "slab": lax.rem(slab + slabs - 1, slabs)}
    sibling = sibling_of(probe, slab)
    partner = partner_of(probe, slab)
    planes = probes_ref.shape[1]
    rows, cols = probes_ref.shape[2], probes_ref.shape[3]
    half = rows // 2
    mine = pl.ds(pl.multiple_of(core * half, half), half)
    other = pl.ds(pl.multiple_of((1 - core) * half, half), half)

    loads = [
        pltpu.make_async_copy(probes_ref, v16.at[:, 2 : planes + 2], load_sems.at[0]),
        pltpu.make_async_copy(change_ref, change.at[2 : planes + 2], load_sems.at[1]),
        pltpu.make_async_copy(pot_ref, pot.at[1 : planes + 1], load_sems.at[2]),
        pltpu.make_async_copy(table_ref, tab, load_sems.at[3]),
    ]
    for load in loads:
        load.start()
    greet([above, below, sibling, partner])
    halo = (halo_s, halo_r)
    copies = [
        remote(change_ref.at[planes - 2 : planes, mine], change.at[0:2, mine], halo, 0, above),
        remote(change_ref.at[0:2, mine], change.at[planes + 2 : planes + 4, mine], halo, 1, below),
        remote(pot_ref.at[planes - 1 : planes, mine], pot.at[0:1, mine], halo, 2, above),
        remote(pot_ref.at[0:1, mine], pot.at[planes + 1 : planes + 2, mine], halo, 3, below),
        remote(probes_ref.at[:, planes - 1 : planes], v16.at[:, 1:2], halo, 4, above),
        remote(probes_ref.at[:, 0:1], v16.at[:, planes + 2 : planes + 3], halo, 5, below),
        remote(probes_ref.at[:, planes - 2 : planes - 1], v16.at[:, 0:1], halo, 6, above),
        remote(probes_ref.at[:, 1:2], v16.at[:, planes + 3 : planes + 4], halo, 7, below),
    ]
    for copy in copies:
        copy.start()
    for load in loads:
        load.wait()

    def chunks(body):
        for index in range(rows // CHUNK):
            body(index * CHUNK)

    lanes = cols // 2
    lane = lax.broadcasted_iota(jnp.int32, (CHUNK, lanes), 1)
    at_low, at_high = lane == 0, lane == lanes - 1

    def seal(buffer, *lead):
        for side in range(2):
            buffer[(*lead, side, pl.ds(0, PAD))] = pltpu.roll(buffer[(*lead, side, pl.ds(rows, PAD))], 1, 0)
            buffer[(*lead, side, pl.ds(rows + PAD, PAD))] = pltpu.roll(buffer[(*lead, side, pl.ds(PAD, PAD))], PAD - 1, 0)

    stretch = rows // 8

    def widen(plane, with_pot):
        for step in range(8):
            here = pl.ds(step * stretch, stretch)
            spread = pl.ds(step, stretch, stride=8)
            inner = pl.ds(PAD + step, stretch, stride=8)
            local = change[plane, here]
            for side in range(2):
                part = slice(side * lanes, (side + 1) * lanes)
                weight[plane, side, spread, :] = local[:, part]
                if with_pot:
                    near[plane - 1, side, spread, :] = pot[plane - 1, here, part]
            for which in range(2):
                value = v16[which, plane, here].astype(F32)
                tangent = value * local
                for side in range(2):
                    part = slice(side * lanes, (side + 1) * lanes)
                    v32[which, plane, side, inner, :] = value[:, part]
                    qbuf[which, plane, side, inner, :] = tangent[:, part]
        for which in range(2):
            seal(v32, which, plane)
            seal(qbuf, which, plane)

    def beside(buffer, which, plane, row):
        inner = pl.ds(row + PAD, CHUNK)
        middle, total = [], []
        for side in range(2):
            wide = buffer[which, plane, side, pl.ds(row, CHUNK + 2 * PAD)]
            middle.append(wide[PAD : PAD + CHUNK])
            around = wide[:CHUNK] + wide[2 * PAD :]
            around = around + (buffer[which, plane - 1, side, inner] + buffer[which, plane + 1, side, inner])
            total.append(around)
        left = [pltpu.roll(value, 1, 1) for value in middle]
        right = [pltpu.roll(value, lanes - 1, 1) for value in middle]
        for side in range(2):
            beyond = jnp.where(at_low, left[1 - side], left[side])
            beyond = beyond + jnp.where(at_high, right[1 - side], right[side])
            total[side] = total[side] + beyond
        return middle, total

    def first(plane):
        def body(row):
            here = pl.ds(row, CHUNK)
            inner = pl.ds(row + PAD, CHUNK)
            for which in range(2):
                terms, around = beside(v32, which, plane + 1, row)
                tangents, beyond = beside(qbuf, which, plane + 1, row)
                for side in range(2):
                    local = near[plane, side, here]
                    term = local * terms[side] - KINETIC * around[side]
                    tbuf[which, plane, side, inner] = term
                    ubuf[which, plane, side, inner] = (
                        local * tangents[side] - KINETIC * beyond[side] + weight[plane + 1, side, here] * term
                    )

        chunks(body)
        for which in range(2):
            seal(tbuf, which, plane)
            seal(ubuf, which, plane)

    mbuf[0:2] = jnp.zeros((2, 24, cols), F32)

    def fold(value):
        total = value[0:8]
        for index in range(1, CHUNK // 8):
            total = total + value[8 * index : 8 * index + 8]
        return total

    def last(plane):
        def body(row):
            here = pl.ds(row, CHUNK)
            inner = pl.ds(row + PAD, CHUNK)
            sums = [None, None]
            for which in range(2):
                terms, around = beside(tbuf, which, plane + 1, row)
                mixes, beyond = beside(ubuf, which, plane + 1, row)
                for side in range(2):
                    local = near[plane + 1, side, here]
                    vector = v32[which, plane + 2, side, inner]
                    tangent = qbuf[which, plane + 2, side, inner]
                    image = local * terms[side] - KINETIC * around[side]
                    third = local * mixes[side] - KINETIC * beyond[side] + weight[plane + 2, side, here] * image
                    parts = (vector * tangent, vector * mixes[side], vector * (4.0 * third - 3.0 * tangent))
                    sums[side] = parts if sums[side] is None else tuple(a + b for a, b in zip(sums[side], parts))
            for side in range(2):
                for order in range(3):
                    mbuf[0, pl.ds(8 * order, 8), side * lanes : (side + 1) * lanes] += fold(sums[side][order])
                dbuf[plane, here, side * lanes : (side + 1) * lanes] = (
                    coef_ref[0] * sums[side][0] + (2.0 * coef_ref[1]) * sums[side][1] + coef_ref[2] * sums[side][2]
                )

        chunks(body)

    def hop_one(plane):
        return remote(ybuf.at[plane, 1 - core], rone.at[plane], (one_s, one_r), plane, sibling)

    def hop_two(plane):
        away = pl.ds(pl.multiple_of((1 - zlow) * half, half), half)
        return remote(ybuf.at[plane, core, away], rtwo.at[plane], (two_s, two_r), plane, partner)

    def transform(plane):
        value = times_table(dbuf[plane], tab.at[0:2])
        value = table_times(tab.at[2:4], value)
        ybuf[plane, 0] = value[:, :lanes]
        ybuf[plane, 1] = value[:, lanes:]
        hop_one(plane).start()

    def merge(plane):
        hop_one(plane).wait_recv()
        ybuf[plane, core] = ybuf[plane, core] + rone[plane]
        hop_two(plane).start()

    def loop(low, high, body):
        def step(index, carry):
            body(index)
            return carry

        lax.fori_loop(low, high, step, 0)

    def settle(plane):
        hop_two(plane).wait_recv()
        value = ybuf[plane, core, keep] + rtwo[plane]
        for row in range(per):
            spread = pl.ds(plane * per + row, slabs, stride=planes * per)
            out_ref[spread, :] = value[row * slabs : (row + 1) * slabs]

    keep = pl.ds(pl.multiple_of(zlow * half, half), half)
    per = half // slabs
    loop(2, planes + 2, functools.partial(widen, with_pot=True))
    loop(2, planes, first)
    loop(2, planes - 2, last)
    loop(2, planes - 2, transform)
    loop(2, planes - 2, merge)
    for copy in copies[:4]:
        copy.wait()
    fwd = (fwd_s, fwd_r)
    forwards = [
        remote(change.at[0:2, mine], change.at[0:2, mine], fwd, 0, sibling),
        remote(change.at[planes + 2 : planes + 4, mine], change.at[planes + 2 : planes + 4, mine], fwd, 1, sibling),
        remote(pot.at[0:1, mine], pot.at[0:1, mine], fwd, 2, sibling),
        remote(pot.at[planes + 1 : planes + 2, mine], pot.at[planes + 1 : planes + 2, mine], fwd, 3, sibling),
    ]
    for copy in forwards:
        copy.start()
    for plane in range(2, planes - 2):
        settle(plane)
    for copy in copies[4:6]:
        copy.wait()
    for copy in forwards:
        copy.wait()

    def both(body, low, high):
        def step(index, carry):
            body(jnp.where(index == 0, low, high))
            return carry

        lax.fori_loop(0, 2, step, 0)

    both(functools.partial(widen, with_pot=True), 1, planes + 2)
    both(first, 1, planes)
    both(last, 1, planes - 2)
    both(transform, 1, planes - 2)
    for copy in copies[6:]:
        copy.wait()
    both(functools.partial(widen, with_pot=False), 0, planes + 3)
    both(merge, 1, planes - 2)
    both(first, 0, planes + 1)
    both(last, 0, planes - 1)

    mom = (mom_s, mom_r)
    for order in range(3):
        strip = jnp.sum(mbuf[0, pl.ds(8 * order, 8)], axis=0, keepdims=True)
        total = jnp.sum(strip, axis=1, keepdims=True)
        mbuf[1, pl.ds(order, 1)] = jnp.broadcast_to(total, (1, cols))
    swap = remote(mbuf.at[1, 0:8], mbuf.at[2, 0:8], mom, 0, sibling)
    swap.start()
    both(transform, 0, planes - 1)
    swap.wait()
    mbuf[3, 0:8] = mbuf[1, 0:8] + mbuf[2, 0:8]
    swap = remote(mbuf.at[3, 0:8], mbuf.at[4, 0:8], mom, 1, partner)
    swap.start()
    both(merge, 0, planes - 1)
    settle(1)
    settle(planes - 2)
    swap.wait()
    moment_ref[...] = (mbuf[3, 0:8] + mbuf[4, 0:8])[:, :128]
    settle(0)
    settle(planes - 1)

    def drain(plane):
        hop_one(plane).wait_send()
        hop_two(plane).wait_send()

    loop(0, planes, drain)


def signed(index, size):
    return jnp.where(index <= size // 2, index, index - size).astype(F32) * (2.0 * math.pi / size)


def solve_kernel(
    slabs, planes, groups,
    ytable_ref, ztable_ref, a_ref, moment_ref,
    out_ref, total_ref,
    ytab, ztab, e_ref, rin, rout, back, far, kern, mslots, load_sems,
    in_s, in_r, out_s, out_r, far_s, far_r, e_s, e_r, mom_s, mom_r,
):
    probe, slab = place()
    core = lax.rem(probe, 2)
    zlow = probe // 2
    sibling = sibling_of(probe, slab)
    partner = partner_of(probe, slab)
    depth = planes * slabs
    rows = ytable_ref.shape[1]
    half = rows // 2
    per = half // slabs
    size = planes * per
    loads = [
        pltpu.make_async_copy(ytable_ref, ytab, load_sems.at[0]),
        pltpu.make_async_copy(ztable_ref, ztab, load_sems.at[1]),
    ]
    for load in loads:
        load.start()
    barrier = pltpu.get_barrier_semaphore()

    def greeting(step, carry):
        peer = {"probe": probe, "slab": lax.rem(slab + step, slabs)}
        pl.semaphore_signal(barrier, inc=1, device_id=peer, device_id_type=MESH)
        return carry

    lax.fori_loop(1, slabs, greeting, 0)
    pl.semaphore_signal(barrier, inc=1, device_id=sibling, device_id_type=MESH)
    pl.semaphore_signal(barrier, inc=1, device_id=partner, device_id_type=MESH)
    pl.semaphore_wait(barrier, slabs + 1)

    def block(index):
        return pl.ds(pl.multiple_of(index * size, size), size)

    def sender(source, target, sems, step):
        peer = lax.rem(slab + step, slabs)
        return remote(source.at[block(peer)], target.at[block(slab)], sems, step, {"probe": probe, "slab": peer})

    def receiver(source, target, sems, step):
        peer = lax.rem(slab + slabs - step, slabs)
        return remote(source.at[block(peer)], target.at[block(peer)], sems, step, {"probe": probe, "slab": peer})

    def exchange_start(source, target, sems):
        def start(step, carry):
            sender(source, target, sems, step).start()
            return carry

        lax.fori_loop(1, slabs, start, 0)
        target[block(slab)] = source[block(slab)]

    def exchange_recv(source, target, sems):
        def finish(step, carry):
            receiver(source, target, sems, step).wait_recv()
            return carry

        lax.fori_loop(1, slabs, finish, 0)

    def exchange_sent(source, target, sems):
        def finish(step, carry):
            sender(source, target, sems, step).wait_send()
            return carry

        lax.fori_loop(1, slabs, finish, 0)

    def moment_round(number):
        stride, count = groups[number]
        where = lax.rem(slab // stride, count)
        copies = []
        for step in range(1, count):
            peer = slab + (lax.rem(where + step, count) - where) * stride
            copies.append(
                remote(
                    mslots.at[number, where], mslots.at[number, where],
                    (mom_s.at[number], mom_r.at[number]), step, {"probe": probe, "slab": peer},
                )
            )
        waits = []
        for step in range(1, count):
            source = lax.rem(where + count - step, count)
            peer = slab + (source - where) * stride
            waits.append(
                remote(
                    mslots.at[number, source], mslots.at[number, source],
                    (mom_s.at[number], mom_r.at[number]), step, {"probe": probe, "slab": peer},
                )
            )
        return where, count, copies, waits

    def moment_start(number, value):
        where, count, copies, waits = moment_round(number)
        mslots[number, where] = value
        for copy in copies:
            copy.start()

    def moment_finish(number):
        where, count, copies, waits = moment_round(number)
        for copy in waits:
            copy.wait_recv()
        for copy in copies:
            copy.wait_send()
        total = mslots[number, 0]
        for index in range(1, count):
            total = total + mslots[number, index]
        return total

    ins, outs = (in_s, in_r), (out_s, out_r)
    exchange_start(a_ref, rin, ins)
    moment_start(0, moment_ref[...])

    wave_z = signed(lax.broadcasted_iota(jnp.int32, (depth, 128), 0), depth)
    wave_x = signed(lax.broadcasted_iota(jnp.int32, (depth, 128), 1) + core * 128, 256)
    base = wave_z * wave_z + wave_x * wave_x
    for row in range(per):
        number = zlow * half + row * slabs + slab
        wave_y = signed(jnp.full((depth, 128), number, jnp.int32), rows)
        summed = base + wave_y * wave_y
        value = (4.0 * math.pi / (8.0 * depth * rows * 256)) / (summed + SCREEN * SCREEN)
        kern[:, row * 128 : (row + 1) * 128] = jnp.where(summed == 0.0, 0.0, value)

    for load in loads:
        load.wait()
    exchange_recv(a_ref, rin, ins)
    moments = moment_finish(0)
    columns = jnp.concatenate([rin[pl.ds(row, depth, stride=per), :] for row in range(per)], axis=1)
    columns = table_times(ztab, columns) * kern[...]
    columns = table_times(ztab, columns)
    for row in range(per):
        rout[pl.ds(row, depth, stride=per), :] = columns[:, row * 128 : (row + 1) * 128]

    exchange_start(rout, back, outs)
    for number in range(1, len(groups)):
        moment_start(number, moments)
        moments = moment_finish(number)
    total_ref[...] = moments
    exchange_recv(rout, back, outs)
    across = remote(back, far, (far_s, far_r), 0, partner)
    across.start()
    across.wait()

    def share(plane):
        return remote(e_ref.at[core, plane], e_ref.at[core, plane], (e_s, e_r), plane, sibling)

    def arrival(plane):
        return remote(e_ref.at[1 - core, plane], e_ref.at[1 - core, plane], (e_s, e_r), plane, sibling)

    for plane in range(planes):
        own = [back[pl.ds(plane * per + row, slabs, stride=size), :] for row in range(per)]
        away = [far[pl.ds(plane * per + row, slabs, stride=size), :] for row in range(per)]
        own = jnp.concatenate(own, axis=0)
        away = jnp.concatenate(away, axis=0)
        low = jnp.where(zlow == 0, own, away)
        high = jnp.where(zlow == 0, away, own)
        e_ref[core, plane] = table_times(ytab, jnp.concatenate([low, high], axis=0))
        share(plane).start()

    def settle(plane, carry):
        arrival(plane).wait_recv()
        share(plane).wait_send()
        value = jnp.concatenate([e_ref[0, plane], e_ref[1, plane]], axis=1)
        out_ref[plane] = times_table(value, ytab)
        return carry

    lax.fori_loop(0, planes, settle, 0)
    exchange_sent(a_ref, rin, ins)
    exchange_sent(rout, back, outs)


def groups_of(slabs):
    return {32: ((1, 4), (4, 2), (8, 4)), 4: ((1, 2), (2, 2))}[slabs]


def per_device(probes, potential, potential_change, coefficients):
    panel, planes, rows, cols = probes.shape
    slabs = lax.axis_size("slab")
    depth = planes * slabs
    half = rows // 2
    per = half // slabs
    vmem = pl.BlockSpec(memory_space=pltpu.VMEM)
    anywhere = pl.BlockSpec(memory_space=pl.ANY)
    dma = pltpu.SemaphoreType.DMA
    high, low = cas_split(rows)
    order = shuffle(rows)
    forward = tables((high, low), (high[:, order], low[:, order]))
    inverse = tables((high, low))
    deep = tables(cas_split(depth))
    tall = rows + 2 * PAD
    spectrum, moments = pl.pallas_call(
        functools.partial(density_kernel, slabs),
        out_shape=(
            jax.ShapeDtypeStruct((planes * half, 128), F32),
            jax.ShapeDtypeStruct((8, 128), F32),
        ),
        in_specs=[pl.BlockSpec(memory_space=pltpu.SMEM), anywhere, anywhere, anywhere, anywhere],
        out_specs=(vmem, vmem),
        scratch_shapes=[
            pltpu.VMEM((4, rows, cols), BF16),
            pltpu.VMEM((panel, planes + 4, rows, cols), BF16),
            pltpu.VMEM((planes + 2, rows, cols), F32),
            pltpu.VMEM((planes + 4, rows, cols), F32),
            pltpu.VMEM((planes + 2, 2, rows, 128), F32),
            pltpu.VMEM((planes + 4, 2, rows, 128), F32),
            pltpu.VMEM((panel, planes + 4, 2, tall, 128), F32),
            pltpu.VMEM((panel, planes + 4, 2, tall, 128), F32),
            pltpu.VMEM((panel, planes + 2, 2, tall, 128), F32),
            pltpu.VMEM((panel, planes + 2, 2, tall, 128), F32),
            pltpu.VMEM((planes, rows, cols), F32),
            pltpu.VMEM((planes, 2, rows, 128), F32),
            pltpu.VMEM((planes, rows, 128), F32),
            pltpu.VMEM((planes, half, 128), F32),
            pltpu.VMEM((5, 24, cols), F32),
            dma((4,)),
            dma((8,)), dma((8,)),
            dma((4,)), dma((4,)),
            dma((planes,)), dma((planes,)),
            dma((planes,)), dma((planes,)),
            dma((2,)), dma((2,)),
        ],
        compiler_params=pltpu.CompilerParams(
            collective_id=0, has_side_effects=True, vmem_limit_bytes=56 * 1024 * 1024
        ),
        name="density",
    )(coefficients, forward, probes, potential, potential_change)
    groups = groups_of(slabs)
    hartree_change, total = pl.pallas_call(
        functools.partial(solve_kernel, slabs, planes, groups),
        out_shape=(
            jax.ShapeDtypeStruct((planes, rows, cols), F32),
            jax.ShapeDtypeStruct((8, 128), F32),
        ),
        in_specs=[anywhere, anywhere, vmem, vmem],
        out_specs=(vmem, vmem),
        scratch_shapes=[
            pltpu.VMEM((2, rows, cols), BF16),
            pltpu.VMEM((2, depth, depth), BF16),
            pltpu.VMEM((2, planes, rows, 128), F32),
            pltpu.VMEM((planes * half, 128), F32),
            pltpu.VMEM((planes * half, 128), F32),
            pltpu.VMEM((planes * half, 128), F32),
            pltpu.VMEM((planes * half, 128), F32),
            pltpu.VMEM((depth, per * 128), F32),
            pltpu.VMEM((len(groups), 4, 8, 128), F32),
            dma((2,)),
            dma((slabs,)), dma((slabs,)),
            dma((slabs,)), dma((slabs,)),
            dma((1,)), dma((1,)),
            dma((planes,)), dma((planes,)),
            dma((len(groups), 4)), dma((len(groups), 4)),
        ],
        compiler_params=pltpu.CompilerParams(
            collective_id=1, has_side_effects=True, vmem_limit_bytes=32 * 1024 * 1024
        ),
        name="solve",
    )(inverse, deep, spectrum, moments)
    weights = jnp.array([1.0, 2.0, 1.0], F32) / (panel * lax.axis_size("probe") * depth * rows * cols)
    return hartree_change, total[:3, 0] * weights


def solution(mesh):
    return jax.shard_map(
        per_device,
        mesh=mesh,
        in_specs=(
            P("probe", "slab", None, None),
            P("slab", None, None),
            P("slab", None, None),
            P(),
        ),
        out_specs=(P("slab", None, None), P()),
        check_vma=False,
    )
```

time: 491 us -> 102 us (0.21); the launches traced: 485 us -> 101 us
  waiting for transfers between devices: 133 us -> 0 us
  Pallas kernels: 0 us -> 96.9 us
  other arithmetic: 92.1 us -> 0.63 us
  blocking collectives: 82.8 us -> 0 us
  matrix products: 79.1 us -> 0 us
  starting transfers between devices: 44.8 us -> 0 us
  local copies, waits for them, and re-layouts: 37.8 us -> 3.05 us
  between operations: 14.6 us -> 0.69 us
    pallas_call x0 -> x2, Pallas kernels: none -> 96.9 us  [the longest x1 52.3 us: per_device(): pl.pallas_call(functools.partial(density_kernel, slabs), out_shape=(jax.S...]
    psum x1 -> x0, blocking collectives: 82.8 us -> none  [record(): local_sum = lax.psum(local_sum, ('probe', 'slab'))]
    dot_general x20 -> x0, matrix products: 79.1 us -> none  [product(): return jnp.einsum(form, left, right, precision=lax.Precision.HIGHEST)]
    psum x1 -> x0, waiting for transfers between devices: 55.2 us -> none  [per_device(): summed = lax.psum(density, 'probe')]
    all_to_all x4 -> x0, waiting for transfers between devices: 53 us -> none  [the longest x1 18.9 us: per_device(): lax.all_to_all(imag_part, 'slab', split_axis=1, concat_axis=0, tiled=True)]
    add x3 -> x0, other arithmetic: 28.7 us -> none  [the longest x2 28.7 us: hamiltonian(): return KINETIC * (6.0 * middle - beside_all) + (potential - CENTRE) * middle]
    all_to_all x4 -> x0, starting transfers between devices: 28.5 us -> none  [the longest x1 9.23 us: per_device(): lax.all_to_all(imag_part, 'slab', split_axis=1, concat_axis=0, tiled=True)]
    another operation x6 -> x0, other arithmetic: 26.4 us -> none  [per_device(): stacked = jnp.stack([current, current_change])]
  transfers between devices with their start and end apart: 11 -> 0, of which waited for: 8 -> 0; matrix products, arithmetic and copies ran while one was open for 14% -> 0% of each run, Pallas kernels for 0% -> 0%
where the time goes in v1:
time: 102 us; the launch traced here: 101 us
  Pallas kernels  96.9 us (95%)
  local copies, waits for them, and re-layouts  3.05 us (3%)
    pallas_call x1, Pallas kernels, per_device(): pl.pallas_call(functools.partial(density_kernel, slabs), out_shape=(jax.S...  52.3 us
    pallas_call x1, Pallas kernels, per_device(): pl.pallas_call(functools.partial(solve_kernel, slabs, planes, groups), ou...  44.6 us
    unnamed x9, local copies, waits for them, and re-layouts  3.05 us

profile of v1, /device:TPU:1, one launch (start us, length us, event | category | flops | bytes accessed | tf_op | source)
XLA Modules:
  0.0 101.2 jit_solution(13268451835427495975)
XLA Ops:
  0.6 0.0 copy-start
  0.6 0.0 copy-start.3
  0.7 52.3 %density.1 = (f32[1024,128]{1,0:T(8,128)}, f32[8,128]{1,0:T(8,128)}) custom-call(f32[3]{0:T(128)} %coef_ref.1, bf16[4,256,256]{2,1,0:T(8,128)(2,1)} %constant.9.clone.table_ref, bf16[2,8,256,256]{3,2,1,0:T(8,128)(2,1)} %probes_ref.1, f32[8,256,256]{2,1,0:T(8,128)} %pot_ref.1, f32[8,256,256]{2,1,0:T(8,128)} %change_ref.1), custom_call_target="tpu_custom_call" | custom-call | tf_op jit(solution)/shard_map/density/pallas_call | solution.py:541
  53.0 0.0 copy-done
  53.0 0.0 copy-start.1
  53.0 1.0 %copy-done.1 = f32[1024,128]{1,0:T(8,128)S(1)} copy-done((f32[1024,128]{1,0:T(8,128)S(1)}, f32[1024,128]{1,0:T(8,128)}, u32[]{:S(2)}) %copy-start.1) | copy-done | bytes 524312
  54.0 0.0 copy-start.2
  54.0 0.7 copy-done.2
  54.7 44.6 %solve.1 = (f32[8,256,256]{2,1,0:T(8,128)S(1)}, f32[8,128]{1,0:T(8,128)S(1)}) custom-call(bf16[2,256,256]{2,1,0:T(8,128)(2,1)S(1)} %copy-done, bf16[2,256,256]{2,1,0:T(8,128)(2,1)S(1)} %copy-done, f32[1024,128]{1,0:T(8,128)S(1)} %copy-done.1, f32[8,128]{1,0:T(8,128)S(1)} %copy-done.2), custom_call_target="tpu_custom_call" | custom-call | tf_op jit(solution)/shard_map/solve/pallas_call | solution.py:578
  99.3 0.0 copy-done.3
  99.3 0.6 multiply_reduce_fusion
  99.9 1.3 %copy.11 = f32[8,256,256]{2,1,0:T(8,128)} copy(f32[8,256,256]{2,1,0:T(8,128)S(1)} %get-tuple-element.12) | data formatting | bytes 4194304
Async XLA Ops:
  0.6 52.3 %copy-start = (bf16[2,256,256]{2,1,0:T(8,128)(2,1)S(1)}, bf16[2,256,256]{2,1,0:T(8,128)(2,1)}, u32[]{:S(2)}) copy-start(bf16[2,256,256]{2,1,0:T(8,128)(2,1)} %constant.10.clone.ytable_ref.ztable_ref) | copy-start | bytes 786436
  0.6 98.6 %copy-start.3 = (f32[3,1]{1,0:T(4,128)S(1)}, f32[3,1]{1,0:T(4,128)}, u32[]{:S(2)}) copy-start(f32[3,1]{1,0:T(4,128)} %constant.16) | copy-start | bytes 40
  53.0 1.0 %copy-start.1 = (f32[1024,128]{1,0:T(8,128)S(1)}, f32[1024,128]{1,0:T(8,128)}, u32[]{:S(2)}) copy-start(f32[1024,128]{1,0:T(8,128)} %get-tuple-element.6.a_ref) | copy-start | bytes 1572868
  54.0 0.7 copy-start.2

commit v2 on v1

--- a/solution.py
+++ b/solution.py
@@ -15,7 +15,6 @@
 BF16 = jnp.bfloat16
 KINETIC = 1.0 / 12.0
 SCREEN = 0.05
-CHUNK = 256
 PAD = 8
 
 
@@ -93,8 +92,9 @@
     slabs,
     coef_ref, table_ref, probes_ref, pot_ref, change_ref,
     out_ref, moment_ref,
-    tab, v16, pot, change, near, weight, v32, qbuf, tbuf, ubuf, dbuf, ybuf, rone, rtwo, mbuf,
-    load_sems, halo_s, halo_r, fwd_s, fwd_r, one_s, one_r, two_s, two_r, mom_s, mom_r,
+    tab, v16, pot, change, ghost_in, near, weight, v32, qbuf, tbuf, ubuf, dbuf,
+    pair_out, pair_in, ybuf, rone, rtwo, mbuf,
+    load_sems, halo_s, halo_r, fwd_s, fwd_r, pair_s, pair_r, one_s, one_r, two_s, two_r, mom_s, mom_r,
 ):
     probe, slab = place()
     core = lax.rem(probe, 2)
@@ -107,12 +107,11 @@
     rows, cols = probes_ref.shape[2], probes_ref.shape[3]
     half = rows // 2
     mine = pl.ds(pl.multiple_of(core * half, half), half)
-    other = pl.ds(pl.multiple_of((1 - core) * half, half), half)
 
     loads = [
-        pltpu.make_async_copy(probes_ref, v16.at[:, 2 : planes + 2], load_sems.at[0]),
-        pltpu.make_async_copy(change_ref, change.at[2 : planes + 2], load_sems.at[1]),
-        pltpu.make_async_copy(pot_ref, pot.at[1 : planes + 1], load_sems.at[2]),
+        pltpu.make_async_copy(change_ref, change, load_sems.at[0]),
+        pltpu.make_async_copy(pot_ref, pot, load_sems.at[1]),
+        pltpu.make_async_copy(probes_ref, v16.at[:, 1 : planes + 1], load_sems.at[2]),
         pltpu.make_async_copy(table_ref, tab, load_sems.at[3]),
     ]
     for load in loads:
@@ -120,27 +119,28 @@
     greet([above, below, sibling, partner])
     halo = (halo_s, halo_r)
     copies = [
-        remote(change_ref.at[planes - 2 : planes, mine], change.at[0:2, mine], halo, 0, above),
-        remote(change_ref.at[0:2, mine], change.at[planes + 2 : planes + 4, mine], halo, 1, below),
-        remote(pot_ref.at[planes - 1 : planes, mine], pot.at[0:1, mine], halo, 2, above),
-        remote(pot_ref.at[0:1, mine], pot.at[planes + 1 : planes + 2, mine], halo, 3, below),
-        remote(probes_ref.at[:, planes - 1 : planes], v16.at[:, 1:2], halo, 4, above),
-        remote(probes_ref.at[:, 0:1], v16.at[:, planes + 2 : planes + 3], halo, 5, below),
-        remote(probes_ref.at[:, planes - 2 : planes - 1], v16.at[:, 0:1], halo, 6, above),
-        remote(probes_ref.at[:, 1:2], v16.at[:, planes + 3 : planes + 4], halo, 7, below),
+        remote(probes_ref.at[:, planes - 1 : planes], v16.at[:, 0:1], halo, 0, above),
+        remote(probes_ref.at[:, 0:1], v16.at[:, planes + 1 : planes + 2], halo, 1, below),
     ]
     for copy in copies:
         copy.start()
+    edges = (
+        (change_ref, planes - 1, above),
+        (change_ref, 0, below),
+        (pot_ref, planes - 1, above),
+        (pot_ref, 0, below),
+    )
+    for index, (field, plane, peer) in enumerate(edges):
+        copy = remote(field.at[plane, mine], ghost_in.at[index, mine], halo, 2 + index, peer)
+        copy.start()
+        copies.append(copy)
     for load in loads:
         load.wait()
 
-    def chunks(body):
-        for index in range(rows // CHUNK):
-            body(index * CHUNK)
-
     lanes = cols // 2
-    lane = lax.broadcasted_iota(jnp.int32, (CHUNK, lanes), 1)
+    lane = lax.broadcasted_iota(jnp.int32, (rows, lanes), 1)
     at_low, at_high = lane == 0, lane == lanes - 1
+    inner = pl.ds(PAD, rows)
 
     def seal(buffer, *lead):
         for side in range(2):
@@ -149,36 +149,38 @@
 
     stretch = rows // 8
 
-    def widen(plane, with_pot):
+    def widen(plane, ghost=None):
         for step in range(8):
             here = pl.ds(step * stretch, stretch)
             spread = pl.ds(step, stretch, stride=8)
-            inner = pl.ds(PAD + step, stretch, stride=8)
-            local = change[plane, here]
+            wide = pl.ds(PAD + step, stretch, stride=8)
+            if ghost is None:
+                local, level = change[plane - 1, here], pot[plane - 1, here]
+            else:
+                local, level = ghost_in[ghost, here], ghost_in[2 + ghost, here]
             for side in range(2):
                 part = slice(side * lanes, (side + 1) * lanes)
                 weight[plane, side, spread, :] = local[:, part]
-                if with_pot:
-                    near[plane - 1, side, spread, :] = pot[plane - 1, here, part]
+                near[plane, side, spread, :] = level[:, part]
             for which in range(2):
                 value = v16[which, plane, here].astype(F32)
                 tangent = value * local
                 for side in range(2):
                     part = slice(side * lanes, (side + 1) * lanes)
-                    v32[which, plane, side, inner, :] = value[:, part]
-                    qbuf[which, plane, side, inner, :] = tangent[:, part]
+                    v32[which, plane, side, wide, :] = value[:, part]
+                    qbuf[which, plane, side, wide, :] = tangent[:, part]
         for which in range(2):
             seal(v32, which, plane)
             seal(qbuf, which, plane)
 
-    def beside(buffer, which, plane, row):
-        inner = pl.ds(row + PAD, CHUNK)
+    def beside(buffer, which, plane, steps):
         middle, total = [], []
         for side in range(2):
-            wide = buffer[which, plane, side, pl.ds(row, CHUNK + 2 * PAD)]
-            middle.append(wide[PAD : PAD + CHUNK])
-            around = wide[:CHUNK] + wide[2 * PAD :]
-            around = around + (buffer[which, plane - 1, side, inner] + buffer[which, plane + 1, side, inner])
+            tall = buffer[which, plane, side]
+            middle.append(tall[PAD : PAD + rows])
+            around = tall[:rows] + tall[2 * PAD :]
+            for step in steps:
+                around = around + buffer[which, plane + step, side, inner]
             total.append(around)
         left = [pltpu.roll(value, 1, 1) for value in middle]
         right = [pltpu.roll(value, lanes - 1, 1) for value in middle]
@@ -188,22 +190,17 @@
             total[side] = total[side] + beyond
         return middle, total
 
-    def first(plane):
-        def body(row):
-            here = pl.ds(row, CHUNK)
-            inner = pl.ds(row + PAD, CHUNK)
-            for which in range(2):
-                terms, around = beside(v32, which, plane + 1, row)
-                tangents, beyond = beside(qbuf, which, plane + 1, row)
-                for side in range(2):
-                    local = near[plane, side, here]
-                    term = local * terms[side] - KINETIC * around[side]
-                    tbuf[which, plane, side, inner] = term
-                    ubuf[which, plane, side, inner] = (
-                        local * tangents[side] - KINETIC * beyond[side] + weight[plane + 1, side, here] * term
-                    )
-
-        chunks(body)
+    def first(plane, steps=(-1, 1)):
+        for which in range(2):
+            terms, around = beside(v32, which, plane, steps)
+            tangents, beyond = beside(qbuf, which, plane, steps)
+            for side in range(2):
+                local = near[plane, side]
+                term = local * terms[side] - KINETIC * around[side]
+                tbuf[which, plane, side, inner] = term
+                ubuf[which, plane, side, inner] = (
+                    local * tangents[side] - KINETIC * beyond[side] + weight[plane, side] * term
+                )
         for which in range(2):
             seal(tbuf, which, plane)
             seal(ubuf, which, plane)
@@ -212,34 +209,42 @@
 
     def fold(value):
         total = value[0:8]
-        for index in range(1, CHUNK // 8):
+        for index in range(1, rows // 8):
             total = total + value[8 * index : 8 * index + 8]
         return total
 
+    def count(order, side, value):
+        mbuf[0, pl.ds(8 * order, 8), side * lanes : (side + 1) * lanes] += fold(value)
+
     def last(plane):
-        def body(row):
-            here = pl.ds(row, CHUNK)
-            inner = pl.ds(row + PAD, CHUNK)
-            sums = [None, None]
-            for which in range(2):
-                terms, around = beside(tbuf, which, plane + 1, row)
-                mixes, beyond = beside(ubuf, which, plane + 1, row)
-                for side in range(2):
-                    local = near[plane + 1, side, here]
-                    vector = v32[which, plane + 2, side, inner]
-                    tangent = qbuf[which, plane + 2, side, inner]
-                    image = local * terms[side] - KINETIC * around[side]
-                    third = local * mixes[side] - KINETIC * beyond[side] + weight[plane + 2, side, here] * image
-                    parts = (vector * tangent, vector * mixes[side], vector * (4.0 * third - 3.0 * tangent))
-                    sums[side] = parts if sums[side] is None else tuple(a + b for a, b in zip(sums[side], parts))
+        sums = [None, None]
+        for which in range(2):
+            terms, around = beside(tbuf, which, plane, (-1, 1))
+            mixes, beyond = beside(ubuf, which, plane, (-1, 1))
             for side in range(2):
-                for order in range(3):
-                    mbuf[0, pl.ds(8 * order, 8), side * lanes : (side + 1) * lanes] += fold(sums[side][order])
-                dbuf[plane, here, side * lanes : (side + 1) * lanes] = (
-                    coef_ref[0] * sums[side][0] + (2.0 * coef_ref[1]) * sums[side][1] + coef_ref[2] * sums[side][2]
-                )
-
-        chunks(body)
+                local = near[plane, side]
+                vector = v32[which, plane, side, inner]
+                tangent = qbuf[which, plane, side, inner]
+                image = local * terms[side] - KINETIC * around[side]
+                third = local * mixes[side] - KINETIC * beyond[side] + weight[plane, side] * image
+                parts = (vector * tangent, vector * mixes[side], vector * (4.0 * third - 3.0 * tangent))
+                sums[side] = parts if sums[side] is None else tuple(a + b for a, b in zip(sums[side], parts))
+        for side in range(2):
+            for order in range(3):
+                count(order, side, sums[side][order])
+            dbuf[plane, :, side * lanes : (side + 1) * lanes] = (
+                coef_ref[0] * sums[side][0] + (2.0 * coef_ref[1]) * sums[side][1] + coef_ref[2] * sums[side][2]
+            )
+
+    def pairs(target, planes_of):
+        low, mid, high = planes_of
+        for side in range(2):
+            product = v32[0, low, side, inner] * v32[0, high, side, inner]
+            product = product + v32[1, low, side, inner] * v32[1, high, side, inner]
+            total = weight[low, side] + weight[mid, side] + weight[high, side]
+            value = (4.0 * KINETIC * KINETIC) * total * product
+            count(2, side, value)
+            pair_out[target, :, side * lanes : (side + 1) * lanes] = (coef_ref[2] * value).astype(BF16)
 
     def hop_one(plane):
         return remote(ybuf.at[plane, 1 - core], rone.at[plane], (one_s, one_r), plane, sibling)
@@ -260,6 +265,16 @@
         ybuf[plane, core] = ybuf[plane, core] + rone[plane]
         hop_two(plane).start()
 
+    keep = pl.ds(pl.multiple_of(zlow * half, half), half)
+    per = half // slabs
+
+    def settle(plane):
+        hop_two(plane).wait_recv()
+        value = ybuf[plane, core, keep] + rtwo[plane]
+        for row in range(per):
+            spread = pl.ds((plane - 1) * per + row, slabs, stride=planes * per)
+            out_ref[spread, :] = value[row * slabs : (row + 1) * slabs]
+
     def loop(low, high, body):
         def step(index, carry):
             body(index)
@@ -267,38 +282,6 @@
 
         lax.fori_loop(low, high, step, 0)
 
-    def settle(plane):
-        hop_two(plane).wait_recv()
-        value = ybuf[plane, core, keep] + rtwo[plane]
-        for row in range(per):
-            spread = pl.ds(plane * per + row, slabs, stride=planes * per)
-            out_ref[spread, :] = value[row * slabs : (row + 1) * slabs]
-
-    keep = pl.ds(pl.multiple_of(zlow * half, half), half)
-    per = half // slabs
-    loop(2, planes + 2, functools.partial(widen, with_pot=True))
-    loop(2, planes, first)
-    loop(2, planes - 2, last)
-    loop(2, planes - 2, transform)
-    loop(2, planes - 2, merge)
-    for copy in copies[:4]:
-        copy.wait()
-    fwd = (fwd_s, fwd_r)
-    forwards = [
-        remote(change.at[0:2, mine], change.at[0:2, mine], fwd, 0, sibling),
-        remote(change.at[planes + 2 : planes + 4, mine], change.at[planes + 2 : planes + 4, mine], fwd, 1, sibling),
-        remote(pot.at[0:1, mine], pot.at[0:1, mine], fwd, 2, sibling),
-        remote(pot.at[planes + 1 : planes + 2, mine], pot.at[planes + 1 : planes + 2, mine], fwd, 3, sibling),
-    ]
-    for copy in forwards:
-        copy.start()
-    for plane in range(2, planes - 2):
-        settle(plane)
-    for copy in copies[4:6]:
-        copy.wait()
-    for copy in forwards:
-        copy.wait()
-
     def both(body, low, high):
         def step(index, carry):
             body(jnp.where(index == 0, low, high))
@@ -306,16 +289,40 @@
 
         lax.fori_loop(0, 2, step, 0)
 
-    both(functools.partial(widen, with_pot=True), 1, planes + 2)
+    loop(1, planes + 1, widen)
+    loop(2, planes, first)
+    loop(3, planes - 1, last)
+    loop(3, planes - 1, transform)
+    loop(3, planes - 1, merge)
+    for copy in copies[2:]:
+        copy.wait()
+    fwd = (fwd_s, fwd_r)
+    forwards = [
+        remote(ghost_in.at[index, mine], ghost_in.at[index, mine], fwd, index, sibling) for index in range(4)
+    ]
+    for copy in forwards:
+        copy.start()
+    for copy in copies[:2]:
+        copy.wait()
+    for copy in forwards:
+        copy.wait()
+    widen(0, 0)
+    widen(planes + 1, 1)
+    pairs(0, (0, 1, 2))
+    pairs(1, (planes - 1, planes, planes + 1))
+    trades = [
+        remote(pair_out.at[0], pair_in.at[1], (pair_s, pair_r), 0, below),
+        remote(pair_out.at[1], pair_in.at[0], (pair_s, pair_r), 1, above),
+    ]
+    for copy in trades:
+        copy.start()
     both(first, 1, planes)
-    both(last, 1, planes - 2)
-    both(transform, 1, planes - 2)
-    for copy in copies[6:]:
-        copy.wait()
-    both(functools.partial(widen, with_pot=False), 0, planes + 3)
-    both(merge, 1, planes - 2)
-    both(first, 0, planes + 1)
-    both(last, 0, planes - 1)
+    both(last, 2, planes - 1)
+    both(transform, 2, planes - 1)
+    first(0, (1,))
+    first(planes + 1, (-1,))
+    both(merge, 2, planes - 1)
+    both(last, 1, planes)
 
     mom = (mom_s, mom_r)
     for order in range(3):
@@ -324,24 +331,30 @@
         mbuf[1, pl.ds(order, 1)] = jnp.broadcast_to(total, (1, cols))
     swap = remote(mbuf.at[1, 0:8], mbuf.at[2, 0:8], mom, 0, sibling)
     swap.start()
-    both(transform, 0, planes - 1)
+    for copy in trades:
+        copy.wait()
+    dbuf[1] += pair_in[0].astype(F32)
+    dbuf[planes] += pair_in[1].astype(F32)
+    both(transform, 1, planes)
+    for plane in range(3, planes - 1):
+        settle(plane)
     swap.wait()
     mbuf[3, 0:8] = mbuf[1, 0:8] + mbuf[2, 0:8]
     swap = remote(mbuf.at[3, 0:8], mbuf.at[4, 0:8], mom, 1, partner)
     swap.start()
-    both(merge, 0, planes - 1)
-    settle(1)
-    settle(planes - 2)
+    both(merge, 1, planes)
+    settle(2)
+    settle(planes - 1)
     swap.wait()
     moment_ref[...] = (mbuf[3, 0:8] + mbuf[4, 0:8])[:, :128]
-    settle(0)
-    settle(planes - 1)
+    settle(1)
+    settle(planes)
 
     def drain(plane):
         hop_one(plane).wait_send()
         hop_two(plane).wait_send()
 
-    loop(0, planes, drain)
+    loop(1, planes + 1, drain)
 
 
 def signed(index, size):
@@ -548,25 +561,29 @@
         out_specs=(vmem, vmem),
         scratch_shapes=[
             pltpu.VMEM((4, rows, cols), BF16),
-            pltpu.VMEM((panel, planes + 4, rows, cols), BF16),
-            pltpu.VMEM((planes + 2, rows, cols), F32),
-            pltpu.VMEM((planes + 4, rows, cols), F32),
+            pltpu.VMEM((panel, planes + 2, rows, cols), BF16),
+            pltpu.VMEM((planes, rows, cols), F32),
+            pltpu.VMEM((planes, rows, cols), F32),
+            pltpu.VMEM((4, rows, cols), F32),
             pltpu.VMEM((planes + 2, 2, rows, 128), F32),
-            pltpu.VMEM((planes + 4, 2, rows, 128), F32),
-            pltpu.VMEM((panel, planes + 4, 2, tall, 128), F32),
-            pltpu.VMEM((panel, planes + 4, 2, tall, 128), F32),
+            pltpu.VMEM((planes + 2, 2, rows, 128), F32),
             pltpu.VMEM((panel, planes + 2, 2, tall, 128), F32),
             pltpu.VMEM((panel, planes + 2, 2, tall, 128), F32),
-            pltpu.VMEM((planes, rows, cols), F32),
-            pltpu.VMEM((planes, 2, rows, 128), F32),
-            pltpu.VMEM((planes, rows, 128), F32),
-            pltpu.VMEM((planes, half, 128), F32),
+            pltpu.VMEM((panel, planes + 2, 2, tall, 128), F32),
+            pltpu.VMEM((panel, planes + 2, 2, tall, 128), F32),
+            pltpu.VMEM((planes + 1, rows, cols), F32),
+            pltpu.VMEM((2, rows, cols), BF16),
+            pltpu.VMEM((2, rows, cols), BF16),
+            pltpu.VMEM((planes + 1, 2, rows, 128), F32),
+            pltpu.VMEM((planes + 1, rows, 128), F32),
+            pltpu.VMEM((planes + 1, half, 128), F32),
             pltpu.VMEM((5, 24, cols), F32),
             dma((4,)),
-            dma((8,)), dma((8,)),
+            dma((6,)), dma((6,)),
             dma((4,)), dma((4,)),
-            dma((planes,)), dma((planes,)),
-            dma((planes,)), dma((planes,)),
+            dma((2,)), dma((2,)),
+            dma((planes + 1,)), dma((planes + 1,)),
+            dma((planes + 1,)), dma((planes + 1,)),
             dma((2,)), dma((2,)),
         ],
         compiler_params=pltpu.CompilerParams(

time: 102 us -> 92 us (0.902)
  the two profiles are of different devices: /device:TPU:1 before, /device:TPU:48 now
where the time goes in v2:
time: 92 us; the launch traced here: 91.8 us
  Pallas kernels  87.4 us (95%)
  local copies, waits for them, and re-layouts  3.05 us (3%)
    pallas_call x1, Pallas kernels, per_device(): pl.pallas_call(functools.partial(solve_kernel, slabs, planes, groups), ou...  50.2 us
    pallas_call x1, Pallas kernels, per_device(): pl.pallas_call(functools.partial(density_kernel, slabs), out_shape=(jax.S...  37.3 us
    unnamed x9, local copies, waits for them, and re-layouts  3.05 us

profile of v2, /device:TPU:48, one launch (start us, length us, event | category | flops | bytes accessed | tf_op | source)
XLA Modules:
  0.0 91.8 jit_solution(13238104210865974619)
XLA Ops:
  0.6 0.0 copy-start
  0.6 0.0 copy-start.3
  0.7 37.3 %density.1 = (f32[1024,128]{1,0:T(8,128)}, f32[8,128]{1,0:T(8,128)}) custom-call(f32[3]{0:T(128)} %coef_ref.1, bf16[4,256,256]{2,1,0:T(8,128)(2,1)} %constant.9.clone.table_ref, bf16[2,8,256,256]{3,2,1,0:T(8,128)(2,1)} %probes_ref.1, f32[8,256,256]{2,1,0:T(8,128)} %pot_ref.1, f32[8,256,256]{2,1,0:T(8,128)} %change_ref.1), custom_call_target="tpu_custom_call" | custom-call | tf_op jit(solution)/shard_map/density/pallas_call | solution.py:554
  37.9 0.0 copy-done
  37.9 0.0 copy-start.1
  37.9 1.0 %copy-done.1 = f32[1024,128]{1,0:T(8,128)S(1)} copy-done((f32[1024,128]{1,0:T(8,128)S(1)}, f32[1024,128]{1,0:T(8,128)}, u32[]{:S(2)}) %copy-start.1) | copy-done | bytes 524312
  39.0 0.0 copy-start.2
  39.0 0.7 copy-done.2
  39.7 50.2 %solve.1 = (f32[8,256,256]{2,1,0:T(8,128)S(1)}, f32[8,128]{1,0:T(8,128)S(1)}) custom-call(bf16[2,256,256]{2,1,0:T(8,128)(2,1)S(1)} %copy-done, bf16[2,256,256]{2,1,0:T(8,128)(2,1)S(1)} %copy-done, f32[1024,128]{1,0:T(8,128)S(1)} %copy-done.1, f32[8,128]{1,0:T(8,128)S(1)} %copy-done.2), custom_call_target="tpu_custom_call" | custom-call | tf_op jit(solution)/shard_map/solve/pallas_call | solution.py:595
  89.9 0.0 copy-done.3
  89.9 0.6 multiply_reduce_fusion
  90.5 1.3 %copy.11 = f32[8,256,256]{2,1,0:T(8,128)} copy(f32[8,256,256]{2,1,0:T(8,128)S(1)} %get-tuple-element.12) | data formatting | bytes 4194304
Async XLA Ops:
  0.6 37.3 %copy-start = (bf16[2,256,256]{2,1,0:T(8,128)(2,1)S(1)}, bf16[2,256,256]{2,1,0:T(8,128)(2,1)}, u32[]{:S(2)}) copy-start(bf16[2,256,256]{2,1,0:T(8,128)(2,1)} %constant.10.clone.ytable_ref.ztable_ref) | copy-start | bytes 786436
  0.6 89.2 %copy-start.3 = (f32[3,1]{1,0:T(4,128)S(1)}, f32[3,1]{1,0:T(4,128)}, u32[]{:S(2)}) copy-start(f32[3,1]{1,0:T(4,128)} %constant.16) | copy-start | bytes 40
  37.9 1.0 %copy-start.1 = (f32[1024,128]{1,0:T(8,128)S(1)}, f32[1024,128]{1,0:T(8,128)}, u32[]{:S(2)}) copy-start(f32[1024,128]{1,0:T(8,128)} %get-tuple-element.6.a_ref) | copy-start | bytes 1572868
  39.0 0.7 copy-start.2

commit v3 on v2

v3 whole, which is shorter than its diff:
```python
import functools
import math

import jax
import jax.numpy as jnp
import ml_dtypes
import numpy as np
from jax import lax
from jax.experimental import pallas as pl
from jax.experimental.pallas import tpu as pltpu
from jax.sharding import PartitionSpec as P

MESH = pl.DeviceIdType.MESH
F32 = jnp.float32
BF16 = jnp.bfloat16
KINETIC = 1.0 / 12.0
SCREEN = 0.05
PAD = 8


def cas_split(size):
    index = np.arange(size)
    angle = (index[:, None] * index[None, :] % size) * (2.0 * np.pi / size)
    table = np.cos(angle) + np.sin(angle)
    high = table.astype(ml_dtypes.bfloat16)
    low = (table - high.astype(np.float64)).astype(ml_dtypes.bfloat16)
    return high, low


def shuffle(size):
    index = np.arange(size)
    return index % 8 * (size // 8) + index // 8


def tables(*pairs):
    return jnp.asarray(np.stack([part for pair in pairs for part in pair]))


def split(value):
    high = value.astype(BF16)
    low = (value - high.astype(F32)).astype(BF16)
    return high, low


def times_table(value, table):
    high, low = split(value)
    total = jnp.dot(high, table[0], preferred_element_type=F32)
    total = total + jnp.dot(high, table[1], preferred_element_type=F32)
    return total + jnp.dot(low, table[0], preferred_element_type=F32)


def table_times(table, value):
    high, low = split(value)
    total = jnp.dot(table[0], high, preferred_element_type=F32)
    total = total + jnp.dot(table[1], high, preferred_element_type=F32)
    return total + jnp.dot(table[0], low, preferred_element_type=F32)


def place():
    probe = lax.axis_index("probe")
    slab = lax.axis_index("slab")
    return probe, slab


def sibling_of(probe, slab):
    return {"probe": probe + 1 - 2 * lax.rem(probe, 2), "slab": slab}


def partner_of(probe, slab):
    return {"probe": lax.rem(probe + 2, 4), "slab": slab}


def greet(peers, count, layer_peer):
    barrier = pltpu.get_barrier_semaphore()
    for peer in peers:
        pl.semaphore_signal(barrier, inc=1, device_id=peer, device_id_type=MESH)

    def signal(step, carry):
        pl.semaphore_signal(barrier, inc=1, device_id=layer_peer(step), device_id_type=MESH)
        return carry

    lax.fori_loop(1, count, signal, 0)
    pl.semaphore_wait(barrier, len(peers) + count - 1)


def remote(source, target, sems, index, peer):
    return pltpu.make_async_remote_copy(
        src_ref=source,
        dst_ref=target,
        send_sem=sems[0].at[index],
        recv_sem=sems[1].at[index],
        device_id=peer,
        device_id_type=MESH,
    )


def signed(index, size):
    return jnp.where(index <= size // 2, index, index - size).astype(F32) * (2.0 * math.pi / size)


def response_kernel(
    slabs, layer,
    coef_ref, table_ref, ztable_ref, probes_ref, pot_ref, change_ref,
    out_ref, moment_ref,
    tab, v16, pot, change, ghost_in, near, weight, v32, qbuf, tbuf, ubuf, dbuf,
    pair_out, pair_in, ybuf, rone, rtwo, gsend, rgate, mbuf,
    ztab, abuf, rin, kern, rout, hold, quads, ebuf, mslots,
    load_sems, halo_s, halo_r, fwd_s, fwd_r, pair_s, pair_r, one_s, one_r, two_s, two_r, gate_s, gate_r, mom_s, mom_r,
    in_s, in_r, out_s, out_r, near_s, near_r, far_s, far_r, relay_s, relay_r, e_s, e_r, mslot_s, mslot_r,
):
    probe, slab = place()
    core = lax.rem(probe, 2)
    zlow = probe // 2
    above = {"probe": probe, "slab": lax.rem(slab + 1, slabs)}
    below = {"probe": probe, "slab": lax.rem(slab + slabs - 1, slabs)}
    sibling = sibling_of(probe, slab)
    partner = partner_of(probe, slab)
    zhigh = lax.rem(slab // 4, 2)
    spot = slab // 8 * 4 + lax.rem(slab, 4)
    across = {"probe": lax.rem(probe + 2, 4), "slab": slab + 4 - 8 * zhigh}

    def spot_after(step):
        return lax.rem(spot + step, layer)

    def layer_peer(step):
        other = spot_after(step)
        return {"probe": probe, "slab": other // 4 * 8 + zhigh * 4 + lax.rem(other, 4)}

    planes = probes_ref.shape[1]
    rows, cols = probes_ref.shape[2], probes_ref.shape[3]
    half = rows // 2
    mine = pl.ds(pl.multiple_of(core * half, half), half)

    loads = [
        pltpu.make_async_copy(change_ref, change, load_sems.at[0]),
        pltpu.make_async_copy(pot_ref, pot, load_sems.at[1]),
        pltpu.make_async_copy(probes_ref, v16.at[:, 1 : planes + 1], load_sems.at[2]),
        pltpu.make_async_copy(table_ref, tab, load_sems.at[3]),
        pltpu.make_async_copy(ztable_ref, ztab, load_sems.at[4]),
    ]
    for load in loads:
        load.start()
    greet([above, below, sibling, partner, across], layer, layer_peer)
    halo = (halo_s, halo_r)
    copies = [
        remote(probes_ref.at[:, planes - 1 : planes], v16.at[:, 0:1], halo, 0, above),
        remote(probes_ref.at[:, 0:1], v16.at[:, planes + 1 : planes + 2], halo, 1, below),
    ]
    for copy in copies:
        copy.start()
    edges = (
        (change_ref, planes - 1, above),
        (change_ref, 0, below),
        (pot_ref, planes - 1, above),
        (pot_ref, 0, below),
    )
    for index, (field, plane, peer) in enumerate(edges):
        copy = remote(field.at[plane, mine], ghost_in.at[index, mine], halo, 2 + index, peer)
        copy.start()
        copies.append(copy)
    for load in loads[:4]:
        load.wait()

    lanes = cols // 2
    lane = lax.broadcasted_iota(jnp.int32, (rows, lanes), 1)
    at_low, at_high = lane == 0, lane == lanes - 1
    inner = pl.ds(PAD, rows)

    def seal(buffer, *lead):
        for side in range(2):
            buffer[(*lead, side, pl.ds(0, PAD))] = pltpu.roll(buffer[(*lead, side, pl.ds(rows, PAD))], 1, 0)
            buffer[(*lead, side, pl.ds(rows + PAD, PAD))] = pltpu.roll(buffer[(*lead, side, pl.ds(PAD, PAD))], PAD - 1, 0)

    stretch = rows // 8

    def widen(plane, ghost=None):
        for step in range(8):
            here = pl.ds(step * stretch, stretch)
            spread = pl.ds(step, stretch, stride=8)
            wide = pl.ds(PAD + step, stretch, stride=8)
            if ghost is None:
                local, level = change[plane - 1, here], pot[plane - 1, here]
            else:
                local, level = ghost_in[ghost, here], ghost_in[2 + ghost, here]
            for side in range(2):
                part = slice(side * lanes, (side + 1) * lanes)
                weight[plane, side, spread, :] = local[:, part]
                near[plane, side, spread, :] = level[:, part]
            for which in range(2):
                value = v16[which, plane, here].astype(F32)
                tangent = value * local
                for side in range(2):
                    part = slice(side * lanes, (side + 1) * lanes)
                    v32[which, plane, side, wide, :] = value[:, part]
                    qbuf[which, plane, side, wide, :] = tangent[:, part]
        for which in range(2):
            seal(v32, which, plane)
            seal(qbuf, which, plane)

    def beside(buffer, which, plane, steps):
        middle, total = [], []
        for side in range(2):
            tall = buffer[which, plane, side]
            middle.append(tall[PAD : PAD + rows])
            around = tall[:rows] + tall[2 * PAD :]
            for step in steps:
                around = around + buffer[which, plane + step, side, inner]
            total.append(around)
        left = [pltpu.roll(value, 1, 1) for value in middle]
        right = [pltpu.roll(value, lanes - 1, 1) for value in middle]
        for side in range(2):
            beyond = jnp.where(at_low, left[1 - side], left[side])
            beyond = beyond + jnp.where(at_high, right[1 - side], right[side])
            total[side] = total[side] + beyond
        return middle, total

    def first(plane, steps=(-1, 1)):
        for which in range(2):
            terms, around = beside(v32, which, plane, steps)
            tangents, beyond = beside(qbuf, which, plane, steps)
            for side in range(2):
                local = near[plane, side]
                term = local * terms[side] - KINETIC * around[side]
                tbuf[which, plane, side, inner] = term
                ubuf[which, plane, side, inner] = (
                    local * tangents[side] - KINETIC * beyond[side] + weight[plane, side] * term
                )
        for which in range(2):
            seal(tbuf, which, plane)
            seal(ubuf, which, plane)

    mbuf[0:2] = jnp.zeros((2, 24, cols), F32)

    def fold(value):
        total = value[0:8]
        for index in range(1, rows // 8):
            total = total + value[8 * index : 8 * index + 8]
        return total

    def count(order, side, value):
        mbuf[0, pl.ds(8 * order, 8), side * lanes : (side + 1) * lanes] += fold(value)

    def last(plane):
        sums = [None, None]
        for which in range(2):
            terms, around = beside(tbuf, which, plane, (-1, 1))
            mixes, beyond = beside(ubuf, which, plane, (-1, 1))
            for side in range(2):
                local = near[plane, side]
                vector = v32[which, plane, side, inner]
                tangent = qbuf[which, plane, side, inner]
                image = local * terms[side] - KINETIC * around[side]
                third = local * mixes[side] - KINETIC * beyond[side] + weight[plane, side] * image
                parts = (vector * tangent, vector * mixes[side], vector * (4.0 * third - 3.0 * tangent))
                sums[side] = parts if sums[side] is None else tuple(a + b for a, b in zip(sums[side], parts))
        for side in range(2):
            for order in range(3):
                count(order, side, sums[side][order])
            dbuf[plane, :, side * lanes : (side + 1) * lanes] = (
                coef_ref[0] * sums[side][0] + (2.0 * coef_ref[1]) * sums[side][1] + coef_ref[2] * sums[side][2]
            )

    def pairs(target, planes_of):
        low, mid, high = planes_of
        for side in range(2):
            product = v32[0, low, side, inner] * v32[0, high, side, inner]
            product = product + v32[1, low, side, inner] * v32[1, high, side, inner]
            total = weight[low, side] + weight[mid, side] + weight[high, side]
            value = (4.0 * KINETIC * KINETIC) * total * product
            count(2, side, value)
            pair_out[target, :, side * lanes : (side + 1) * lanes] = (coef_ref[2] * value).astype(BF16)

    def hop_one(plane):
        return remote(ybuf.at[plane, 1 - core], rone.at[plane], (one_s, one_r), plane, sibling)

    fourth = rows // 4
    per = fourth // layer
    depth = planes * slabs
    size = 2 * planes * per

    def quarter(low, high):
        return pl.ds(pl.multiple_of((2 * low + high) * fourth, fourth), fourth)

    def hop_two(plane):
        return remote(
            ybuf.at[plane, core, quarter(1 - zlow, zhigh)], rtwo.at[plane, 0], (two_s.at[0], two_r.at[0]), plane, partner
        )

    def hop_pass(plane):
        return remote(
            ybuf.at[plane, core, quarter(zlow, 1 - zhigh)], rtwo.at[plane, 1], (two_s.at[1], two_r.at[1]), plane, partner
        )

    def hop_gate(plane):
        return remote(gsend.at[plane], rgate.at[plane], (gate_s, gate_r), plane, across)

    def transform(group):
        count = len(group)
        value = jnp.concatenate([dbuf[plane] for plane in group], axis=0)
        value = times_table(value, tab.at[0:2])
        value = jnp.concatenate([value[index * rows : (index + 1) * rows] for index in range(count)], axis=1)
        value = table_times(tab.at[2:4], value)
        for index, plane in enumerate(group):
            ybuf[plane, 0] = value[:, index * cols : index * cols + lanes]
            ybuf[plane, 1] = value[:, index * cols + lanes : (index + 1) * cols]
            hop_one(plane).start()

    def merge(plane):
        hop_one(plane).wait_recv()
        ybuf[plane, core] = ybuf[plane, core] + rone[plane]
        hop_pass(plane).start()
        hop_two(plane).start()

    def relay(plane):
        hop_pass(plane).wait_recv()
        gsend[plane] = ybuf[plane, core, quarter(1 - zlow, 1 - zhigh)] + rtwo[plane, 1]
        hop_gate(plane).start()

    inside = list(range(3, planes - 1))
    outside = [1, 2, planes - 1, planes]

    def spread(plane, which, value):
        group = inside if plane in inside else outside
        first_row = (0 if plane in inside else size // 2) + group.index(plane) * per
        for row in range(per):
            start = first_row + which * (size // 4) + row
            abuf[pl.ds(start, layer, stride=size), :] = value[row * layer : (row + 1) * layer]

    def settle(plane):
        hop_two(plane).wait_recv()
        spread(plane, zhigh, ybuf[plane, core, quarter(zlow, zhigh)] + rtwo[plane, 0])

    def collect(plane):
        hop_gate(plane).wait_recv()
        spread(plane, 1 - zhigh, rgate[plane])

    def in_rows(place_of, piece):
        return pl.ds(pl.multiple_of(place_of * size + piece * (size // 2), size // 2), size // 2)

    def in_copy(step, piece, here):
        rows_at = in_rows(spot_after(step), piece)
        return remote(abuf.at[rows_at], rin.at[here], (in_s.at[piece], in_r.at[piece]), step, layer_peer(step))

    def in_start(piece):
        def start(step, carry):
            in_copy(step, piece, in_rows(spot, piece)).start()
            return carry

        lax.fori_loop(1, layer, start, 0)
        rin[in_rows(spot, piece)] = abuf[in_rows(spot, piece)]

    def in_finish(piece):
        def finish(step, carry):
            in_copy(step, piece, in_rows(spot_after(layer - step), piece)).wait_recv()
            return carry

        lax.fori_loop(1, layer, finish, 0)

    def loop(low, high, body):
        def step(index, carry):
            body(index)
            return carry

        lax.fori_loop(low, high, step, 0)

    def both(body, low, high):
        def step(index, carry):
            body(jnp.where(index == 0, low, high))
            return carry

        lax.fori_loop(0, 2, step, 0)

    loop(1, planes + 1, widen)
    loop(2, planes, first)
    loop(3, planes - 1, last)
    transform(inside)
    loop(3, planes - 1, merge)
    for copy in copies[2:]:
        copy.wait()
    fwd = (fwd_s, fwd_r)
    forwards = [
        remote(ghost_in.at[index, mine], ghost_in.at[index, mine], fwd, index, sibling) for index in range(4)
    ]
    for copy in forwards:
        copy.start()
    loop(3, planes - 1, relay)
    for copy in copies[:2]:
        copy.wait()
    for copy in forwards:
        copy.wait()
    widen(0, 0)
    widen(planes + 1, 1)
    pairs(0, (0, 1, 2))
    pairs(1, (planes - 1, planes, planes + 1))
    trades = [
        remote(pair_out.at[0], pair_in.at[1], (pair_s, pair_r), 0, below),
        remote(pair_out.at[1], pair_in.at[0], (pair_s, pair_r), 1, above),
    ]
    for copy in trades:
        copy.start()
    both(first, 1, planes)
    for plane in inside:
        settle(plane)
    both(last, 2, planes - 1)
    transform([2, planes - 1])
    for plane in inside:
        collect(plane)
    in_start(0)
    first(0, (1,))
    first(planes + 1, (-1,))
    both(merge, 2, planes - 1)
    both(last, 1, planes)

    mom = (mom_s, mom_r)
    for order in range(3):
        strip = jnp.sum(mbuf[0, pl.ds(8 * order, 8)], axis=0, keepdims=True)
        total = jnp.sum(strip, axis=1, keepdims=True)
        mbuf[1, pl.ds(order, 1)] = jnp.broadcast_to(total, (1, cols))
    swap = remote(mbuf.at[1, 0:8], mbuf.at[2, 0:8], mom, 0, sibling)
    swap.start()
    both(relay, 2, planes - 1)
    for copy in trades:
        copy.wait()
    dbuf[1] += pair_in[0].astype(F32)
    dbuf[planes] += pair_in[1].astype(F32)
    transform([1, planes])
    settle(2)
    settle(planes - 1)
    swap.wait()
    mbuf[3, 0:8] = mbuf[1, 0:8] + mbuf[2, 0:8]
    swap = remote(mbuf.at[3, 0:8], mbuf.at[4, 0:8], mom, 1, partner)
    swap.start()
    both(merge, 1, planes)
    both(relay, 1, planes)
    collect(2)
    collect(planes - 1)
    settle(1)
    settle(planes)
    collect(1)
    collect(planes)
    in_start(1)
    swap.wait()
    mbuf[5, 0:8] = mbuf[3, 0:8] + mbuf[4, 0:8]
    swap = remote(mbuf.at[5, 0:8], mbuf.at[6, 0:8], mom, 2, across)
    swap.start()

    wave_z = signed(lax.broadcasted_iota(jnp.int32, (depth, lanes), 0), depth)
    wave_x = signed(lax.broadcasted_iota(jnp.int32, (depth, lanes), 1) + core * lanes, cols)
    base = wave_z * wave_z + wave_x * wave_x
    for row in range(per):
        number = (2 * zlow + zhigh) * fourth + row * layer + spot
        wave_y = signed(jnp.full((depth, lanes), number, jnp.int32), rows)
        summed = base + wave_y * wave_y
        value = (4.0 * math.pi / (8.0 * depth * rows * cols)) / (summed + SCREEN * SCREEN)
        kern[:, row * lanes : (row + 1) * lanes] = jnp.where(summed == 0.0, 0.0, value)
    loads[4].wait()

    def moment_round(number, stride):
        where = lax.rem(slab // stride, 4)
        copies, waits = [], []
        for step in range(1, 4):
            peer = {"probe": probe, "slab": slab + (lax.rem(where + step, 4) - where) * stride}
            source = lax.rem(where + 4 - step, 4)
            sems = (mslot_s.at[number], mslot_r.at[number])
            copies.append(remote(mslots.at[number, where], mslots.at[number, where], sems, step, peer))
            waits.append(remote(mslots.at[number, source], mslots.at[number, source], sems, step, peer))
        return where, copies, waits

    def moment_start(number, stride, value):
        where, copies, waits = moment_round(number, stride)
        mslots[number, where] = value
        for copy in copies:
            copy.start()

    def moment_finish(number, stride):
        where, copies, waits = moment_round(number, stride)
        for copy in waits:
            copy.wait_recv()
        for copy in copies:
            copy.wait_send()
        return (mslots[number, 0] + mslots[number, 1]) + (mslots[number, 2] + mslots[number, 3])

    in_finish(0)
    swap.wait()
    moment_start(0, 1, (mbuf[5, 0:8] + mbuf[6, 0:8])[:, :128])
    in_finish(1)
    columns = jnp.concatenate([rin[pl.ds(row, depth, stride=per), :] for row in range(per)], axis=1)
    here = lax.broadcasted_iota(jnp.int32, (1, per * lanes), 1) + (probe + slab) * (per * lanes)
    mean = jnp.sum(columns, axis=0, keepdims=True) * (1.0 / depth)
    columns = columns - jnp.where(here == 0, mean, 0.0)
    columns = table_times(ztab.at[0:2], columns) * kern[...]
    columns = table_times(ztab.at[2:4], columns)
    for row in range(per):
        rout[pl.ds(row, depth, stride=per), :] = columns[:, row * lanes : (row + 1) * lanes]

    piece = planes // 2 * per
    own_quarter = 2 * zlow + zhigh
    far_quarter = 2 * (1 - zlow) + (1 - zhigh)

    def out_rows(place_of, side, part):
        which = zhigh if side == 0 else 1 - zhigh
        return pl.ds(pl.multiple_of(place_of * size + which * (size // 2) + part * piece, piece), piece)

    def landing(side, part, place_of):
        rows_at = pl.ds(pl.multiple_of(place_of * piece, piece), piece)
        return quads.at[own_quarter, part, rows_at] if side == 0 else hold.at[part, rows_at]

    def out_copy(step, side, part, place_of):
        source = rout.at[out_rows(spot_after(step), side, part)]
        sems = (out_s.at[side, part], out_r.at[side, part])
        return remote(source, landing(side, part, place_of), sems, step, layer_peer(step))

    def out_start(side, part):
        def start(step, carry):
            out_copy(step, side, part, spot).start()
            return carry

        lax.fori_loop(1, layer, start, 0)
        target = landing(side, part, spot)
        target[...] = rout[out_rows(spot, side, part)]

    def out_finish(side, part):
        def finish(step, carry):
            out_copy(step, side, part, spot_after(layer - step)).wait_recv()
            return carry

        lax.fori_loop(1, layer, finish, 0)

    def to_partner(part):
        return remote(quads.at[own_quarter, part], quads.at[own_quarter, part], (near_s, near_r), part, partner)

    def to_across(part):
        return remote(hold.at[part], quads.at[own_quarter, part], (far_s, far_r), part, across)

    def pass_on(part):
        return remote(quads.at[far_quarter, part], quads.at[far_quarter, part], (relay_s, relay_r), part, partner)

    for part in range(2):
        out_start(0, part)
        out_start(1, part)
    moments = moment_finish(0, 1)
    moment_start(1, 8, moments)
    for part in range(2):
        out_finish(0, part)
        to_partner(part).start()
        out_finish(1, part)
        to_across(part).start()
    moment_ref[...] = moment_finish(1, 8)
    for part in range(2):
        to_across(part).wait_recv()
        pass_on(part).start()

    def share(part):
        return remote(ebuf.at[core, part], ebuf.at[core, part], (e_s, e_r), part, sibling)

    def invert(part):
        to_partner(part).wait_recv()
        pass_on(part).wait_recv()
        columns = []
        for plane in range(planes // 2):
            blocks = [
                quads[which, part, pl.ds(plane * per + row, layer, stride=piece), :]
                for which in range(4)
                for row in range(per)
            ]
            columns.append(jnp.concatenate(blocks, axis=0))
        ebuf[core, part] = table_times(tab.at[0:2], jnp.concatenate(columns, axis=1))
        share(part).start()

    def finish(part):
        share(part).wait_recv()
        value = [
            jnp.concatenate([ebuf[side, part, :, plane * lanes : (plane + 1) * lanes] for side in range(2)], axis=1)
            for plane in range(planes // 2)
        ]
        value = times_table(jnp.concatenate(value, axis=0), tab.at[0:2])
        for plane in range(planes // 2):
            out_ref[part * (planes // 2) + plane] = value[plane * rows : (plane + 1) * rows]

    invert(0)
    finish(0)
    invert(1)
    finish(1)

    def drain(plane):
        hop_one(plane).wait_send()
        hop_two(plane).wait_send()
        hop_pass(plane).wait_send()
        hop_gate(plane).wait_send()

    loop(1, planes + 1, drain)

    def sent(step, carry):
        for part in range(2):
            in_copy(step, part, in_rows(spot, part)).wait_send()
            for side in range(2):
                out_copy(step, side, part, spot).wait_send()
        return carry

    lax.fori_loop(1, layer, sent, 0)
    for part in range(2):
        to_partner(part).wait_send()
        to_across(part).wait_send()
        pass_on(part).wait_send()
        share(part).wait_send()


def per_device(probes, potential, potential_change, coefficients):
    panel, planes, rows, cols = probes.shape
    slabs = lax.axis_size("slab")
    layer = slabs // 2
    depth = planes * slabs
    fourth = rows // 4
    size = 2 * planes * (fourth // layer)
    vmem = pl.BlockSpec(memory_space=pltpu.VMEM)
    anywhere = pl.BlockSpec(memory_space=pl.ANY)
    dma = pltpu.SemaphoreType.DMA
    high, low = cas_split(rows)
    order = shuffle(rows)
    forward = tables((high, low), (high[:, order], low[:, order]))
    high, low = cas_split(depth)
    spots = np.arange(layer)[:, None, None, None] // 4 * 8 + np.arange(layer)[:, None, None, None] % 4
    halves = np.arange(2)[None, None, :, None] * 4
    inner = np.array([list(range(2, planes - 2)), [0, 1, planes - 2, planes - 1]])[None, :, None, :]
    came = ((spots + halves) * planes + inner).reshape(-1)
    goes = ((spots[:, 0] + halves[:, 0]) * planes + np.arange(planes)).reshape(-1)
    deep = tables((high[:, came], low[:, came]), (high[goes], low[goes]))
    tall = rows + 2 * PAD
    hartree_change, total = pl.pallas_call(
        functools.partial(response_kernel, slabs, layer),
        out_shape=(
            jax.ShapeDtypeStruct((planes, rows, cols), F32),
            jax.ShapeDtypeStruct((8, 128), F32),
        ),
        in_specs=[pl.BlockSpec(memory_space=pltpu.SMEM)] + [anywhere] * 5,
        out_specs=(vmem, vmem),
        scratch_shapes=[
            pltpu.VMEM((4, rows, cols), BF16),
            pltpu.VMEM((panel, planes + 2, rows, cols), BF16),
            pltpu.VMEM((planes, rows, cols), F32),
            pltpu.VMEM((planes, rows, cols), F32),
            pltpu.VMEM((4, rows, cols), F32),
            pltpu.VMEM((planes + 2, 2, rows, 128), F32),
            pltpu.VMEM((planes + 2, 2, rows, 128), F32),
            pltpu.VMEM((panel, planes + 2, 2, tall, 128), F32),
            pltpu.VMEM((panel, planes + 2, 2, tall, 128), F32),
            pltpu.VMEM((panel, planes + 2, 2, tall, 128), F32),
            pltpu.VMEM((panel, planes + 2, 2, tall, 128), F32),
            pltpu.VMEM((planes + 1, rows, cols), F32),
            pltpu.VMEM((2, rows, cols), BF16),
            pltpu.VMEM((2, rows, cols), BF16),
            pltpu.VMEM((planes + 1, 2, rows, 128), F32),
            pltpu.VMEM((planes + 1, rows, 128), F32),
            pltpu.VMEM((planes + 1, 2, fourth, 128), F32),
            pltpu.VMEM((planes + 1, fourth, 128), F32),
            pltpu.VMEM((planes + 1, fourth, 128), F32),
            pltpu.VMEM((7, 24, cols), F32),
            pltpu.VMEM((4, depth, depth), BF16),
            pltpu.VMEM((layer * size, 128), F32),
            pltpu.VMEM((layer * size, 128), F32),
            pltpu.VMEM((depth, 4 * 128), F32),
            pltpu.VMEM((layer * size, 128), F32),
            pltpu.VMEM((2, layer * size // 4, 128), F32),
            pltpu.VMEM((4, 2, layer * size // 4, 128), F32),
            pltpu.VMEM((2, 2, rows, planes // 2 * 128), F32),
            pltpu.VMEM((2, 4, 8, 128), F32),
            dma((5,)),
            dma((6,)), dma((6,)),
            dma((4,)), dma((4,)),
            dma((2,)), dma((2,)),
            dma((planes + 1,)), dma((planes + 1,)),
            dma((2, planes + 1)), dma((2, planes + 1)),
            dma((planes + 1,)), dma((planes + 1,)),
            dma((3,)), dma((3,)),
            dma((2, layer)), dma((2, layer)),
            dma((2, 2, layer)), dma((2, 2, layer)),
            dma((2,)), dma((2,)),
            dma((2,)), dma((2,)),
            dma((2,)), dma((2,)),
            dma((2,)), dma((2,)),
            dma((2, 4)), dma((2, 4)),
        ],
        compiler_params=pltpu.CompilerParams(
            collective_id=0, has_side_effects=True, vmem_limit_bytes=60 * 1024 * 1024
        ),
        name="response",
    )(coefficients, forward, deep, probes, potential, potential_change)
    weights = jnp.array([1.0, 2.0, 1.0], F32) / (panel * lax.axis_size("probe") * depth * rows * cols)
    return hartree_change, total[:3, 0] * weights


def solution(mesh):
    return jax.shard_map(
        per_device,
        mesh=mesh,
        in_specs=(
            P("probe", "slab", None, None),
            P("slab", None, None),
            P("slab", None, None),
            P(),
        ),
        out_specs=(P("slab", None, None), P()),
        check_vma=False,
    )
```

time: 92 us -> 90.4 us (0.983)
  the two profiles are of different devices: /device:TPU:48 before, /device:TPU:1 now
where the time goes in v3:
time: 90.4 us; the launch traced here: 90.2 us
  Pallas kernels  85.2 us (94%)
  local copies, waits for them, and re-layouts  3.05 us (3%)
  other arithmetic  1.31 us (1%)
    pallas_call x1, Pallas kernels, per_device(): pl.pallas_call(functools.partial(response_kernel, slabs, layer), out_shap...  85.2 us
    unnamed x3, local copies, waits for them, and re-layouts  3.05 us

profile of v3, /device:TPU:1, one launch (start us, length us, event | category | flops | bytes accessed | tf_op | source)
XLA Modules:
  0.0 90.2 jit_solution(2502748804094307229)
XLA Ops:
  0.6 0.0 copy-start
  0.6 85.2 %response.1 = (f32[8,256,256]{2,1,0:T(8,128)}, f32[8,128]{1,0:T(8,128)}) custom-call(f32[3]{0:T(128)} %coef_ref.1, bf16[4,256,256]{2,1,0:T(8,128)(2,1)} %constant.9.clone.table_ref, bf16[4,256,256]{2,1,0:T(8,128)(2,1)} %constant.10.clone.ztable_ref, bf16[2,8,256,256]{3,2,1,0:T(8,128)(2,1)} %probes_ref.1, f32[8,256,256]{2,1,0:T(8,128)} %pot_ref.1, ...), custom_call_target="tpu_custom_call" | custom-call | tf_op jit(solution)/shard_map/response/pallas_call | solution.py:629
  85.9 0.0 copy-done
  85.9 1.3 %multiply_reduce_fusion = f32[3]{0:T(128)} fusion(f32[3,1]{1,0:T(4,128)S(1)} %copy-done, f32[8,128]{1,0:T(8,128)} %get-tuple-element.5), kind=kLoop, calls=%fused_computation | loop fusion | flops 3 | bytes 36 | tf_op jit(solution)/shard_map/mul | solution.py:689
  87.2 3.0 %copy.10 = f32[8,256,256]{2,1,0:T(8,128)} copy(f32[8,256,256]{2,1,0:T(8,128)} %get-tuple-element.8) | data formatting | bytes 4194304
Async XLA Ops:
  0.6 85.2 %copy-start = (f32[3,1]{1,0:T(4,128)S(1)}, f32[3,1]{1,0:T(4,128)}, u32[]{:S(2)}) copy-start(f32[3,1]{1,0:T(4,128)} %constant.16) | copy-start | bytes 40

commit v4 on v3

--- a/solution.py
+++ b/solution.py
@@ -70,17 +70,11 @@
     return {"probe": lax.rem(probe + 2, 4), "slab": slab}
 
 
-def greet(peers, count, layer_peer):
+def greet(peers):
     barrier = pltpu.get_barrier_semaphore()
     for peer in peers:
         pl.semaphore_signal(barrier, inc=1, device_id=peer, device_id_type=MESH)
-
-    def signal(step, carry):
-        pl.semaphore_signal(barrier, inc=1, device_id=layer_peer(step), device_id_type=MESH)
-        return carry
-
-    lax.fori_loop(1, count, signal, 0)
-    pl.semaphore_wait(barrier, len(peers) + count - 1)
+    pl.semaphore_wait(barrier, len(peers))
 
 
 def remote(source, target, sems, index, peer):
@@ -103,10 +97,10 @@
     coef_ref, table_ref, ztable_ref, probes_ref, pot_ref, change_ref,
     out_ref, moment_ref,
     tab, v16, pot, change, ghost_in, near, weight, v32, qbuf, tbuf, ubuf, dbuf,
-    pair_out, pair_in, ybuf, rone, rtwo, gsend, rgate, mbuf,
-    ztab, abuf, rin, kern, rout, hold, quads, ebuf, mslots,
-    load_sems, halo_s, halo_r, fwd_s, fwd_r, pair_s, pair_r, one_s, one_r, two_s, two_r, gate_s, gate_r, mom_s, mom_r,
-    in_s, in_r, out_s, out_r, near_s, near_r, far_s, far_r, relay_s, relay_r, e_s, e_r, mslot_s, mslot_r,
+    pair_out, pair_in, ybuf, rone, rtwo, mbuf,
+    ztab, abuf, rin, kern, rout, hold, quads, mslots,
+    load_sems, halo_s, halo_r, fwd_s, fwd_r, pair_s, pair_r, one_s, one_r, two_s, two_r, mom_s, mom_r,
+    in_s, in_r, out_s, out_r, near_s, near_r, far_s, far_r, relay_s, relay_r, e_s, e_r, mslot_s, mslot_r, ready,
 ):
     probe, slab = place()
     core = lax.rem(probe, 2)
@@ -126,6 +120,13 @@
         other = spot_after(step)
         return {"probe": probe, "slab": other // 4 * 8 + zhigh * 4 + lax.rem(other, 4)}
 
+    def other_peer(step):
+        other = spot_after(step)
+        return {
+            "probe": lax.rem(probe + 2, 4),
+            "slab": other // 4 * 8 + (1 - zhigh) * 4 + lax.rem(other, 4),
+        }
+
     planes = probes_ref.shape[1]
     rows, cols = probes_ref.shape[2], probes_ref.shape[3]
     half = rows // 2
@@ -140,7 +141,11 @@
     ]
     for load in loads:
         load.start()
-    greet([above, below, sibling, partner, across], layer, layer_peer)
+    column = [{"probe": probe, "slab": slab - lax.rem(slab, 4) + lax.rem(slab + step, 4)} for step in range(1, 4)]
+    row_peers = [{"probe": probe, "slab": lax.rem(slab + 8 * step, slabs)} for step in range(1, 4)]
+    greet([above, below, sibling, partner, across] + column + row_peers)
+    for peer in row_peers:
+        pl.semaphore_signal(ready.at[0], inc=1, device_id=peer, device_id_type=MESH)
     halo = (halo_s, halo_r)
     copies = [
         remote(probes_ref.at[:, planes - 1 : planes], v16.at[:, 0:1], halo, 0, above),
@@ -291,9 +296,6 @@
             ybuf.at[plane, core, quarter(zlow, 1 - zhigh)], rtwo.at[plane, 1], (two_s.at[1], two_r.at[1]), plane, partner
         )
 
-    def hop_gate(plane):
-        return remote(gsend.at[plane], rgate.at[plane], (gate_s, gate_r), plane, across)
-
     def transform(group):
         count = len(group)
         value = jnp.concatenate([dbuf[plane] for plane in group], axis=0)
@@ -311,50 +313,60 @@
         hop_pass(plane).start()
         hop_two(plane).start()
 
+    inside = list(range(3, planes - 1))
+    outside = [1, 2, planes - 1, planes]
+
+    def spread(plane, side, value):
+        group = inside if plane in inside else outside
+        first_row = (0 if plane in inside else size // 4) + group.index(plane) * per
+        for row in range(per):
+            abuf[side, pl.ds(first_row + row, layer, stride=size // 2), :] = value[row * layer : (row + 1) * layer]
+
     def relay(plane):
         hop_pass(plane).wait_recv()
-        gsend[plane] = ybuf[plane, core, quarter(1 - zlow, 1 - zhigh)] + rtwo[plane, 1]
-        hop_gate(plane).start()
-
-    inside = list(range(3, planes - 1))
-    outside = [1, 2, planes - 1, planes]
-
-    def spread(plane, which, value):
-        group = inside if plane in inside else outside
-        first_row = (0 if plane in inside else size // 2) + group.index(plane) * per
-        for row in range(per):
-            start = first_row + which * (size // 4) + row
-            abuf[pl.ds(start, layer, stride=size), :] = value[row * layer : (row + 1) * layer]
+        spread(plane, 1, ybuf[plane, core, quarter(1 - zlow, 1 - zhigh)] + rtwo[plane, 1])
 
     def settle(plane):
         hop_two(plane).wait_recv()
-        spread(plane, zhigh, ybuf[plane, core, quarter(zlow, zhigh)] + rtwo[plane, 0])
-
-    def collect(plane):
-        hop_gate(plane).wait_recv()
-        spread(plane, 1 - zhigh, rgate[plane])
-
-    def in_rows(place_of, piece):
-        return pl.ds(pl.multiple_of(place_of * size + piece * (size // 2), size // 2), size // 2)
-
-    def in_copy(step, piece, here):
-        rows_at = in_rows(spot_after(step), piece)
-        return remote(abuf.at[rows_at], rin.at[here], (in_s.at[piece], in_r.at[piece]), step, layer_peer(step))
-
-    def in_start(piece):
+        spread(plane, 0, ybuf[plane, core, quarter(zlow, zhigh)] + rtwo[plane, 0])
+
+    def in_from(place_of, piece):
+        return pl.ds(pl.multiple_of(place_of * (size // 2) + piece * (size // 4), size // 4), size // 4)
+
+    def in_rows(place_of, piece, which):
+        start = place_of * size + piece * (size // 2) + which * (size // 4)
+        return pl.ds(pl.multiple_of(start, size // 4), size // 4)
+
+    def in_copy(step, piece, side, here):
+        source = abuf.at[side, in_from(spot_after(step), piece)]
+        peer = layer_peer(step) if side == 0 else other_peer(step)
+        return remote(source, rin.at[here], (in_s.at[piece, side], in_r.at[piece, side]), step, peer)
+
+    def in_start(piece, side):
         def start(step, carry):
-            in_copy(step, piece, in_rows(spot, piece)).start()
+            in_copy(step, piece, side, in_rows(spot, piece, zhigh)).start()
             return carry
 
-        lax.fori_loop(1, layer, start, 0)
-        rin[in_rows(spot, piece)] = abuf[in_rows(spot, piece)]
+        lax.fori_loop(1 - side, layer, start, 0)
+        if side == 0:
+            rin[in_rows(spot, piece, zhigh)] = abuf[0, in_from(spot, piece)]
+
+    def in_sent(piece, side):
+        def finish(step, carry):
+            in_copy(step, piece, side, in_rows(spot, piece, zhigh)).wait_send()
+            return carry
+
+        lax.fori_loop(1 - side, layer, finish, 0)
 
     def in_finish(piece):
-        def finish(step, carry):
-            in_copy(step, piece, in_rows(spot_after(layer - step), piece)).wait_recv()
-            return carry
-
-        lax.fori_loop(1, layer, finish, 0)
+        for side in range(2):
+            def finish(step, carry):
+                place_of = lax.rem(spot + layer - step, layer)
+                which = zhigh if side == 0 else 1 - zhigh
+                in_copy(step, piece, side, in_rows(place_of, piece, which)).wait_recv()
+                return carry
+
+            lax.fori_loop(1 - side, layer, finish, 0)
 
     def loop(low, high, body):
         def step(index, carry):
@@ -383,7 +395,15 @@
     ]
     for copy in forwards:
         copy.start()
-    loop(3, planes - 1, relay)
+    pl.semaphore_wait(ready.at[0], 3)
+    pl.semaphore_signal(ready.at[1], inc=1, device_id=across, device_id_type=MESH)
+    for plane in inside:
+        relay(plane)
+    pl.semaphore_wait(ready.at[1], 1)
+    in_start(0, 1)
+    for plane in inside:
+        settle(plane)
+    in_start(0, 0)
     for copy in copies[:2]:
         copy.wait()
     for copy in forwards:
@@ -399,17 +419,17 @@
     for copy in trades:
         copy.start()
     both(first, 1, planes)
-    for plane in inside:
-        settle(plane)
     both(last, 2, planes - 1)
     transform([2, planes - 1])
-    for plane in inside:
-        collect(plane)
-    in_start(0)
     first(0, (1,))
     first(planes + 1, (-1,))
     both(merge, 2, planes - 1)
     both(last, 1, planes)
+    for copy in trades:
+        copy.wait()
+    dbuf[1] += pair_in[0].astype(F32)
+    dbuf[planes] += pair_in[1].astype(F32)
+    transform([1, planes])
 
     mom = (mom_s, mom_r)
     for order in range(3):
@@ -418,27 +438,20 @@
         mbuf[1, pl.ds(order, 1)] = jnp.broadcast_to(total, (1, cols))
     swap = remote(mbuf.at[1, 0:8], mbuf.at[2, 0:8], mom, 0, sibling)
     swap.start()
-    both(relay, 2, planes - 1)
-    for copy in trades:
-        copy.wait()
-    dbuf[1] += pair_in[0].astype(F32)
-    dbuf[planes] += pair_in[1].astype(F32)
-    transform([1, planes])
-    settle(2)
-    settle(planes - 1)
+    for plane in (2, planes - 1):
+        relay(plane)
+        settle(plane)
+    both(merge, 1, planes)
     swap.wait()
     mbuf[3, 0:8] = mbuf[1, 0:8] + mbuf[2, 0:8]
     swap = remote(mbuf.at[3, 0:8], mbuf.at[4, 0:8], mom, 1, partner)
     swap.start()
-    both(merge, 1, planes)
-    both(relay, 1, planes)
-    collect(2)
-    collect(planes - 1)
+    relay(1)
+    relay(planes)
+    in_start(1, 1)
     settle(1)
     settle(planes)
-    collect(1)
-    collect(planes)
-    in_start(1)
+    in_start(1, 0)
     swap.wait()
     mbuf[5, 0:8] = mbuf[3, 0:8] + mbuf[4, 0:8]
     swap = remote(mbuf.at[5, 0:8], mbuf.at[6, 0:8], mom, 2, across)
@@ -526,6 +539,15 @@
 
         lax.fori_loop(1, layer, finish, 0)
 
+    def out_sent():
+        def finish(step, carry):
+            for side in range(2):
+                for part in range(2):
+                    out_copy(step, side, part, spot).wait_send()
+            return carry
+
+        lax.fori_loop(1, layer, finish, 0)
+
     def to_partner(part):
         return remote(quads.at[own_quarter, part], quads.at[own_quarter, part], (near_s, near_r), part, partner)
 
@@ -540,6 +562,16 @@
         out_start(1, part)
     moments = moment_finish(0, 1)
     moment_start(1, 8, moments)
+
+    def drain(plane):
+        hop_one(plane).wait_send()
+        hop_two(plane).wait_send()
+        hop_pass(plane).wait_send()
+
+    loop(1, planes + 1, drain)
+    for piece_number in range(2):
+        for side in range(2):
+            in_sent(piece_number, side)
     for part in range(2):
         out_finish(0, part)
         to_partner(part).start()
@@ -551,7 +583,8 @@
         pass_on(part).start()
 
     def share(part):
-        return remote(ebuf.at[core, part], ebuf.at[core, part], (e_s, e_r), part, sibling)
+        slot = pl.ds(4 * core + 2 * part, 2)
+        return remote(pot.at[slot], pot.at[slot], (e_s, e_r), part, sibling)
 
     def invert(part):
         to_partner(part).wait_recv()
@@ -564,13 +597,18 @@
                 for row in range(per)
             ]
             columns.append(jnp.concatenate(blocks, axis=0))
-        ebuf[core, part] = table_times(tab.at[0:2], jnp.concatenate(columns, axis=1))
+        value = table_times(tab.at[0:2], jnp.concatenate(columns, axis=1))
+        for pair in range(2):
+            pot[4 * core + 2 * part + pair] = value[:, pair * cols : (pair + 1) * cols]
         share(part).start()
 
     def finish(part):
         share(part).wait_recv()
         value = [
-            jnp.concatenate([ebuf[side, part, :, plane * lanes : (plane + 1) * lanes] for side in range(2)], axis=1)
+            jnp.concatenate(
+                [pot[4 * side + 2 * part + plane // 2, :, plane % 2 * lanes : (plane % 2 + 1) * lanes] for side in range(2)],
+                axis=1,
+            )
             for plane in range(planes // 2)
         ]
         value = times_table(jnp.concatenate(value, axis=0), tab.at[0:2])
@@ -579,25 +617,9 @@
 
     invert(0)
     finish(0)
+    out_sent()
     invert(1)
     finish(1)
-
-    def drain(plane):
-        hop_one(plane).wait_send()
-        hop_two(plane).wait_send()
-        hop_pass(plane).wait_send()
-        hop_gate(plane).wait_send()
-
-    loop(1, planes + 1, drain)
-
-    def sent(step, carry):
-        for part in range(2):
-            in_copy(step, part, in_rows(spot, part)).wait_send()
-            for side in range(2):
-                out_copy(step, side, part, spot).wait_send()
-        return carry
-
-    lax.fori_loop(1, layer, sent, 0)
     for part in range(2):
         to_partner(part).wait_send()
         to_across(part).wait_send()
@@ -629,7 +651,7 @@
     hartree_change, total = pl.pallas_call(
         functools.partial(response_kernel, slabs, layer),
         out_shape=(
-            jax.ShapeDtypeStruct((planes, rows, cols), F32),
+            pltpu.VMEM((planes, rows, cols), F32),
             jax.ShapeDtypeStruct((8, 128), F32),
         ),
         in_specs=[pl.BlockSpec(memory_space=pltpu.SMEM)] + [anywhere] * 5,
@@ -652,17 +674,14 @@
             pltpu.VMEM((planes + 1, 2, rows, 128), F32),
             pltpu.VMEM((planes + 1, rows, 128), F32),
             pltpu.VMEM((planes + 1, 2, fourth, 128), F32),
-            pltpu.VMEM((planes + 1, fourth, 128), F32),
-            pltpu.VMEM((planes + 1, fourth, 128), F32),
             pltpu.VMEM((7, 24, cols), F32),
             pltpu.VMEM((4, depth, depth), BF16),
-            pltpu.VMEM((layer * size, 128), F32),
+            pltpu.VMEM((2, layer * size // 2, 128), F32),
             pltpu.VMEM((layer * size, 128), F32),
             pltpu.VMEM((depth, 4 * 128), F32),
             pltpu.VMEM((layer * size, 128), F32),
             pltpu.VMEM((2, layer * size // 4, 128), F32),
             pltpu.VMEM((4, 2, layer * size // 4, 128), F32),
-            pltpu.VMEM((2, 2, rows, planes // 2 * 128), F32),
             pltpu.VMEM((2, 4, 8, 128), F32),
             dma((5,)),
             dma((6,)), dma((6,)),
@@ -670,18 +689,18 @@
             dma((2,)), dma((2,)),
             dma((planes + 1,)), dma((planes + 1,)),
             dma((2, planes + 1)), dma((2, planes + 1)),
-            dma((planes + 1,)), dma((planes + 1,)),
             dma((3,)), dma((3,)),
-            dma((2, layer)), dma((2, layer)),
+            dma((2, 2, layer)), dma((2, 2, layer)),
             dma((2, 2, layer)), dma((2, 2, layer)),
             dma((2,)), dma((2,)),
             dma((2,)), dma((2,)),
             dma((2,)), dma((2,)),
             dma((2,)), dma((2,)),
             dma((2, 4)), dma((2, 4)),
+            pltpu.SemaphoreType.REGULAR((2,)),
         ],
         compiler_params=pltpu.CompilerParams(
-            collective_id=0, has_side_effects=True, vmem_limit_bytes=60 * 1024 * 1024
+            collective_id=0, has_side_effects=True, vmem_limit_bytes=56 * 1024 * 1024
         ),
         name="response",
     )(coefficients, forward, deep, probes, potential, potential_change)

time: 90.4 us -> 82.9 us (0.917)
  Pallas kernels: 85.2 us -> 80.1 us
  local copies, waits for them, and re-layouts: 3.05 us -> 1.33 us
    pallas_call x1, Pallas kernels: 85.2 us -> 80.1 us  [per_device(): pl.pallas_call(functools.partial(response_kernel, slabs, layer), out_shap...]
    unnamed x3 -> x5, local copies, waits for them, and re-layouts: 3.05 us -> 1.33 us
where the time goes in v4:
time: 82.9 us; the launch traced here: 82.7 us
  Pallas kernels  80.1 us (97%)
  local copies, waits for them, and re-layouts  1.33 us (2%)
    pallas_call x1, Pallas kernels, per_device(): pl.pallas_call(functools.partial(response_kernel, slabs, layer), out_shap...  80.1 us

profile of v4, /device:TPU:1, one launch (start us, length us, event | category | flops | bytes accessed | tf_op | source)
XLA Modules:
  0.0 82.7 jit_solution(765526520080091548)
XLA Ops:
  0.6 80.1 %response.1 = (f32[8,256,256]{2,1,0:T(8,128)S(1)}, f32[8,128]{1,0:T(8,128)}) custom-call(f32[3]{0:T(128)} %coef_ref.1, bf16[4,256,256]{2,1,0:T(8,128)(2,1)} %constant.9.clone.table_ref, bf16[4,256,256]{2,1,0:T(8,128)(2,1)} %constant.10.clone.ztable_ref, bf16[2,8,256,256]{3,2,1,0:T(8,128)(2,1)} %probes_ref.1, f32[8,256,256]{2,1,0:T(8,128)} %pot_ref.1, ...), custom_call_target="tpu_custom_call" | custom-call | tf_op jit(solution)/shard_map/response/pallas_call | solution.py:651
  80.8 0.0 copy-start
  80.8 0.0 copy-start.1
  80.8 1.3 %copy.10 = f32[8,256,256]{2,1,0:T(8,128)} copy(f32[8,256,256]{2,1,0:T(8,128)S(1)} %get-tuple-element.6) | data formatting | bytes 4194304
  82.1 0.0 copy-done
  82.1 0.0 copy-done.1
  82.1 0.6 multiply_reduce_fusion
Async XLA Ops:
  80.8 1.3 %copy-start = (f32[3,1]{1,0:T(4,128)S(1)}, f32[3,1]{1,0:T(4,128)}, u32[]{:S(2)}) copy-start(f32[3,1]{1,0:T(4,128)} %constant.16) | copy-start | bytes 40
  80.8 1.3 %copy-start.1 = (f32[8,128]{1,0:T(8,128)S(1)}, f32[8,128]{1,0:T(8,128)}, u32[]{:S(2)}) copy-start(f32[8,128]{1,0:T(8,128)} %get-tuple-element.5) | copy-start | bytes 12292

commit v5 on v4

--- a/solution.py
+++ b/solution.py
@@ -16,6 +16,7 @@
 KINETIC = 1.0 / 12.0
 SCREEN = 0.05
 PAD = 8
+STEP = 16
 
 
 def cas_split(size):
@@ -167,7 +168,7 @@
         load.wait()
 
     lanes = cols // 2
-    lane = lax.broadcasted_iota(jnp.int32, (rows, lanes), 1)
+    lane = lax.broadcasted_iota(jnp.int32, (STEP, lanes), 1)
     at_low, at_high = lane == 0, lane == lanes - 1
     inner = pl.ds(PAD, rows)
 
@@ -202,14 +203,14 @@
             seal(v32, which, plane)
             seal(qbuf, which, plane)
 
-    def beside(buffer, which, plane, steps):
+    def beside(buffer, which, plane, row, steps):
         middle, total = [], []
         for side in range(2):
-            tall = buffer[which, plane, side]
-            middle.append(tall[PAD : PAD + rows])
-            around = tall[:rows] + tall[2 * PAD :]
+            tall = buffer[which, plane, side, row : row + STEP + 2 * PAD]
+            middle.append(tall[PAD : PAD + STEP])
+            around = tall[:STEP] + tall[2 * PAD :]
             for step in steps:
-                around = around + buffer[which, plane + step, side, inner]
+                around = around + buffer[which, plane + step, side, row + PAD : row + PAD + STEP]
             total.append(around)
         left = [pltpu.roll(value, 1, 1) for value in middle]
         right = [pltpu.roll(value, lanes - 1, 1) for value in middle]
@@ -220,16 +221,19 @@
         return middle, total
 
     def first(plane, steps=(-1, 1)):
-        for which in range(2):
-            terms, around = beside(v32, which, plane, steps)
-            tangents, beyond = beside(qbuf, which, plane, steps)
-            for side in range(2):
-                local = near[plane, side]
-                term = local * terms[side] - KINETIC * around[side]
-                tbuf[which, plane, side, inner] = term
-                ubuf[which, plane, side, inner] = (
-                    local * tangents[side] - KINETIC * beyond[side] + weight[plane, side] * term
-                )
+        for row in range(0, rows, STEP):
+            here = slice(row, row + STEP)
+            there = slice(row + PAD, row + PAD + STEP)
+            for which in range(2):
+                terms, around = beside(v32, which, plane, row, steps)
+                tangents, beyond = beside(qbuf, which, plane, row, steps)
+                for side in range(2):
+                    local = near[plane, side, here]
+                    term = local * terms[side] - KINETIC * around[side]
+                    tbuf[which, plane, side, there] = term
+                    ubuf[which, plane, side, there] = (
+                        local * tangents[side] - KINETIC * beyond[side] + weight[plane, side, here] * term
+                    )
         for which in range(2):
             seal(tbuf, which, plane)
             seal(ubuf, which, plane)
@@ -238,7 +242,7 @@
 
     def fold(value):
         total = value[0:8]
-        for index in range(1, rows // 8):
+        for index in range(1, value.shape[0] // 8):
             total = total + value[8 * index : 8 * index + 8]
         return total
 
@@ -246,24 +250,31 @@
         mbuf[0, pl.ds(8 * order, 8), side * lanes : (side + 1) * lanes] += fold(value)
 
     def last(plane):
-        sums = [None, None]
-        for which in range(2):
-            terms, around = beside(tbuf, which, plane, (-1, 1))
-            mixes, beyond = beside(ubuf, which, plane, (-1, 1))
+        tallies = [[0.0] * 3, [0.0] * 3]
+        for row in range(0, rows, STEP):
+            here = slice(row, row + STEP)
+            there = slice(row + PAD, row + PAD + STEP)
+            sums = [None, None]
+            for which in range(2):
+                terms, around = beside(tbuf, which, plane, row, (-1, 1))
+                mixes, beyond = beside(ubuf, which, plane, row, (-1, 1))
+                for side in range(2):
+                    local = near[plane, side, here]
+                    vector = v32[which, plane, side, there]
+                    tangent = qbuf[which, plane, side, there]
+                    image = local * terms[side] - KINETIC * around[side]
+                    third = local * mixes[side] - KINETIC * beyond[side] + weight[plane, side, here] * image
+                    parts = (vector * tangent, vector * mixes[side], vector * (4.0 * third - 3.0 * tangent))
+                    sums[side] = parts if sums[side] is None else tuple(a + b for a, b in zip(sums[side], parts))
             for side in range(2):
-                local = near[plane, side]
-                vector = v32[which, plane, side, inner]
-                tangent = qbuf[which, plane, side, inner]
-                image = local * terms[side] - KINETIC * around[side]
-                third = local * mixes[side] - KINETIC * beyond[side] + weight[plane, side] * image
-                parts = (vector * tangent, vector * mixes[side], vector * (4.0 * third - 3.0 * tangent))
-                sums[side] = parts if sums[side] is None else tuple(a + b for a, b in zip(sums[side], parts))
+                for order in range(3):
+                    tallies[side][order] = tallies[side][order] + fold(sums[side][order])
+                dbuf[plane, here, side * lanes : (side + 1) * lanes] = (
+                    coef_ref[0] * sums[side][0] + (2.0 * coef_ref[1]) * sums[side][1] + coef_ref[2] * sums[side][2]
+                )
         for side in range(2):
             for order in range(3):
-                count(order, side, sums[side][order])
-            dbuf[plane, :, side * lanes : (side + 1) * lanes] = (
-                coef_ref[0] * sums[side][0] + (2.0 * coef_ref[1]) * sums[side][1] + coef_ref[2] * sums[side][2]
-            )
+                mbuf[0, pl.ds(8 * order, 8), side * lanes : (side + 1) * lanes] += tallies[side][order]
 
     def pairs(target, planes_of):
         low, mid, high = planes_of
@@ -397,13 +408,6 @@
         copy.start()
     pl.semaphore_wait(ready.at[0], 3)
     pl.semaphore_signal(ready.at[1], inc=1, device_id=across, device_id_type=MESH)
-    for plane in inside:
-        relay(plane)
-    pl.semaphore_wait(ready.at[1], 1)
-    in_start(0, 1)
-    for plane in inside:
-        settle(plane)
-    in_start(0, 0)
     for copy in copies[:2]:
         copy.wait()
     for copy in forwards:
@@ -421,9 +425,16 @@
     both(first, 1, planes)
     both(last, 2, planes - 1)
     transform([2, planes - 1])
+    for plane in inside:
+        relay(plane)
+    pl.semaphore_wait(ready.at[1], 1)
+    in_start(0, 1)
+    both(merge, 2, planes - 1)
+    for plane in inside:
+        settle(plane)
+    in_start(0, 0)
     first(0, (1,))
     first(planes + 1, (-1,))
-    both(merge, 2, planes - 1)
     both(last, 1, planes)
     for copy in trades:
         copy.wait()

time: 82.9 us -> 80.3 us (0.969)
  Pallas kernels: 80.1 us -> 77.6 us
    pallas_call x1, Pallas kernels: 80.1 us -> 77.6 us  [per_device(): pl.pallas_call(functools.partial(response_kernel, slabs, layer), out_shap...]
where the time goes in v5:
time: 80.3 us; the launch traced here: 80.2 us
  Pallas kernels  77.6 us (97%)
  local copies, waits for them, and re-layouts  1.33 us (2%)
    pallas_call x1, Pallas kernels, per_device(): pl.pallas_call(functools.partial(response_kernel, slabs, layer), out_shap...  77.6 us

profile of v5, /device:TPU:1, one launch (start us, length us, event | category | flops | bytes accessed | tf_op | source)
XLA Modules:
  0.0 80.2 jit_solution(7785800420697872040)
XLA Ops:
  0.6 77.6 %response.1 = (f32[8,256,256]{2,1,0:T(8,128)S(1)}, f32[8,128]{1,0:T(8,128)}) custom-call(f32[3]{0:T(128)} %coef_ref.1, bf16[4,256,256]{2,1,0:T(8,128)(2,1)} %constant.9.clone.table_ref, bf16[4,256,256]{2,1,0:T(8,128)(2,1)} %constant.10.clone.ztable_ref, bf16[2,8,256,256]{3,2,1,0:T(8,128)(2,1)} %probes_ref.1, f32[8,256,256]{2,1,0:T(8,128)} %pot_ref.1, ...), custom_call_target="tpu_custom_call" | custom-call | tf_op jit(solution)/shard_map/response/pallas_call | solution.py:662
  78.2 0.0 copy-start
  78.2 0.0 copy-start.1
  78.2 1.3 %copy.10 = f32[8,256,256]{2,1,0:T(8,128)} copy(f32[8,256,256]{2,1,0:T(8,128)S(1)} %get-tuple-element.6) | data formatting | bytes 4194304
  79.6 0.0 copy-done
  79.6 0.0 copy-done.1
  79.6 0.6 multiply_reduce_fusion
Async XLA Ops:
  78.2 1.3 %copy-start = (f32[3,1]{1,0:T(4,128)S(1)}, f32[3,1]{1,0:T(4,128)}, u32[]{:S(2)}) copy-start(f32[3,1]{1,0:T(4,128)} %constant.16) | copy-start | bytes 40
  78.2 1.3 %copy-start.1 = (f32[8,128]{1,0:T(8,128)S(1)}, f32[8,128]{1,0:T(8,128)}, u32[]{:S(2)}) copy-start(f32[8,128]{1,0:T(8,128)} %get-tuple-element.5) | copy-start | bytes 12292

commit v6 on v5

--- a/solution.py
+++ b/solution.py
@@ -97,10 +97,10 @@
     slabs, layer,
     coef_ref, table_ref, ztable_ref, probes_ref, pot_ref, change_ref,
     out_ref, moment_ref,
-    tab, v16, pot, change, ghost_in, near, weight, v32, qbuf, tbuf, ubuf, dbuf,
-    pair_out, pair_in, ybuf, rone, rtwo, mbuf,
+    tab, v16, pot, change, ghost_in, level_out, level_in, near, weight, v32, qbuf, tbuf, ubuf, dbuf,
+    ybuf, rone, rtwo, mbuf,
     ztab, abuf, rin, kern, rout, hold, quads, mslots,
-    load_sems, halo_s, halo_r, fwd_s, fwd_r, pair_s, pair_r, one_s, one_r, two_s, two_r, mom_s, mom_r,
+    load_sems, halo_s, halo_r, fwd_s, fwd_r, one_s, one_r, two_s, two_r, mom_s, mom_r,
     in_s, in_r, out_s, out_r, near_s, near_r, far_s, far_r, relay_s, relay_r, e_s, e_r, mslot_s, mslot_r, ready,
 ):
     probe, slab = place()
@@ -154,18 +154,15 @@
     ]
     for copy in copies:
         copy.start()
-    edges = (
-        (change_ref, planes - 1, above),
-        (change_ref, 0, below),
-        (pot_ref, planes - 1, above),
-        (pot_ref, 0, below),
-    )
-    for index, (field, plane, peer) in enumerate(edges):
-        copy = remote(field.at[plane, mine], ghost_in.at[index, mine], halo, 2 + index, peer)
-        copy.start()
-        copies.append(copy)
+    for index, (plane, peer) in enumerate(((planes - 1, above), (0, below))):
+        copies.append(remote(change_ref.at[plane, mine], ghost_in.at[index, mine], halo, 2 + index, peer))
+        copies[-1].start()
     for load in loads[:4]:
         load.wait()
+    for index, (plane, peer) in enumerate(((planes - 1, above), (0, below))):
+        level_out[index] = pot[plane, mine].astype(BF16)
+        copies.append(remote(level_out.at[index], level_in.at[index, mine], halo, 4 + index, peer))
+        copies[-1].start()
 
     lanes = cols // 2
     lane = lax.broadcasted_iota(jnp.int32, (STEP, lanes), 1)
@@ -184,14 +181,12 @@
             here = pl.ds(step * stretch, stretch)
             spread = pl.ds(step, stretch, stride=8)
             wide = pl.ds(PAD + step, stretch, stride=8)
-            if ghost is None:
-                local, level = change[plane - 1, here], pot[plane - 1, here]
-            else:
-                local, level = ghost_in[ghost, here], ghost_in[2 + ghost, here]
+            local = change[plane - 1, here] if ghost is None else ghost_in[ghost, here]
             for side in range(2):
                 part = slice(side * lanes, (side + 1) * lanes)
                 weight[plane, side, spread, :] = local[:, part]
-                near[plane, side, spread, :] = level[:, part]
+                if ghost is None:
+                    near[plane, side, spread, :] = pot[plane - 1, here, part]
             for which in range(2):
                 value = v16[which, plane, here].astype(F32)
                 tangent = value * local
@@ -202,6 +197,13 @@
         for which in range(2):
             seal(v32, which, plane)
             seal(qbuf, which, plane)
+
+    def level(plane, ghost):
+        for step in range(8):
+            for side in range(2):
+                part = slice(side * lanes, (side + 1) * lanes)
+                value = level_in[ghost, step * stretch : (step + 1) * stretch, part].astype(F32)
+                near[plane, side, pl.ds(step, stretch, stride=8), :] = value
 
     def beside(buffer, which, plane, row, steps):
         middle, total = [], []
@@ -284,7 +286,7 @@
             total = weight[low, side] + weight[mid, side] + weight[high, side]
             value = (4.0 * KINETIC * KINETIC) * total * product
             count(2, side, value)
-            pair_out[target, :, side * lanes : (side + 1) * lanes] = (coef_ref[2] * value).astype(BF16)
+            dbuf[target, :, side * lanes : (side + 1) * lanes] = coef_ref[2] * value
 
     def hop_one(plane):
         return remote(ybuf.at[plane, 1 - core], rone.at[plane], (one_s, one_r), plane, sibling)
@@ -325,13 +327,15 @@
         hop_two(plane).start()
 
     inside = list(range(3, planes - 1))
-    outside = [1, 2, planes - 1, planes]
+    outside = [0, planes + 1, 1, 2, planes - 1, planes]
+    pieces = ((0, len(inside) * per), (len(inside) * per, len(outside) * per))
+    sent_rows = (planes + 2) * per
 
     def spread(plane, side, value):
         group = inside if plane in inside else outside
-        first_row = (0 if plane in inside else size // 4) + group.index(plane) * per
+        first_row = (0 if plane in inside else pieces[1][0]) + group.index(plane) * per
         for row in range(per):
-            abuf[side, pl.ds(first_row + row, layer, stride=size // 2), :] = value[row * layer : (row + 1) * layer]
+            abuf[side, pl.ds(first_row + row, layer, stride=sent_rows), :] = value[row * layer : (row + 1) * layer]
 
     def relay(plane):
         hop_pass(plane).wait_recv()
@@ -342,11 +346,12 @@
         spread(plane, 0, ybuf[plane, core, quarter(zlow, zhigh)] + rtwo[plane, 0])
 
     def in_from(place_of, piece):
-        return pl.ds(pl.multiple_of(place_of * (size // 2) + piece * (size // 4), size // 4), size // 4)
+        start, length = pieces[piece]
+        return pl.ds(pl.multiple_of(place_of * sent_rows + start, 8), length)
 
     def in_rows(place_of, piece, which):
-        start = place_of * size + piece * (size // 2) + which * (size // 4)
-        return pl.ds(pl.multiple_of(start, size // 4), size // 4)
+        start, length = pieces[piece]
+        return pl.ds(pl.multiple_of(place_of * (2 * sent_rows) + 2 * start + which * length, 8), length)
 
     def in_copy(step, piece, side, here):
         source = abuf.at[side, in_from(spot_after(step), piece)]
@@ -393,19 +398,20 @@
 
         lax.fori_loop(0, 2, step, 0)
 
+    fwd = (fwd_s, fwd_r)
+    forwards = [
+        remote(ghosts.at[index, mine], ghosts.at[index, mine], fwd, number * 2 + index, sibling)
+        for number, ghosts in enumerate((ghost_in, level_in))
+        for index in range(2)
+    ]
     loop(1, planes + 1, widen)
     loop(2, planes, first)
     loop(3, planes - 1, last)
-    transform(inside)
-    loop(3, planes - 1, merge)
     for copy in copies[2:]:
         copy.wait()
-    fwd = (fwd_s, fwd_r)
-    forwards = [
-        remote(ghost_in.at[index, mine], ghost_in.at[index, mine], fwd, index, sibling) for index in range(4)
-    ]
     for copy in forwards:
         copy.start()
+    transform(inside)
     pl.semaphore_wait(ready.at[0], 3)
     pl.semaphore_signal(ready.at[1], inc=1, device_id=across, device_id_type=MESH)
     for copy in copies[:2]:
@@ -415,14 +421,11 @@
     widen(0, 0)
     widen(planes + 1, 1)
     pairs(0, (0, 1, 2))
-    pairs(1, (planes - 1, planes, planes + 1))
-    trades = [
-        remote(pair_out.at[0], pair_in.at[1], (pair_s, pair_r), 0, below),
-        remote(pair_out.at[1], pair_in.at[0], (pair_s, pair_r), 1, above),
-    ]
-    for copy in trades:
-        copy.start()
+    pairs(planes + 1, (planes - 1, planes, planes + 1))
+    loop(3, planes - 1, merge)
+    transform([0, planes + 1])
     both(first, 1, planes)
+    both(merge, 0, planes + 1)
     both(last, 2, planes - 1)
     transform([2, planes - 1])
     for plane in inside:
@@ -433,13 +436,11 @@
     for plane in inside:
         settle(plane)
     in_start(0, 0)
+    level(0, 0)
+    level(planes + 1, 1)
     first(0, (1,))
     first(planes + 1, (-1,))
     both(last, 1, planes)
-    for copy in trades:
-        copy.wait()
-    dbuf[1] += pair_in[0].astype(F32)
-    dbuf[planes] += pair_in[1].astype(F32)
     transform([1, planes])
 
     mom = (mom_s, mom_r)
@@ -449,7 +450,7 @@
         mbuf[1, pl.ds(order, 1)] = jnp.broadcast_to(total, (1, cols))
     swap = remote(mbuf.at[1, 0:8], mbuf.at[2, 0:8], mom, 0, sibling)
     swap.start()
-    for plane in (2, planes - 1):
+    for plane in (0, planes + 1, 2, planes - 1):
         relay(plane)
         settle(plane)
     both(merge, 1, planes)
@@ -508,12 +509,17 @@
     swap.wait()
     moment_start(0, 1, (mbuf[5, 0:8] + mbuf[6, 0:8])[:, :128])
     in_finish(1)
-    columns = jnp.concatenate([rin[pl.ds(row, depth, stride=per), :] for row in range(per)], axis=1)
+    came = 2 * (planes + 2) * layer
+    columns = jnp.concatenate([rin[pl.ds(row, came, stride=per), :] for row in range(per)], axis=1)
     here = lax.broadcasted_iota(jnp.int32, (1, per * lanes), 1) + (probe + slab) * (per * lanes)
-    mean = jnp.sum(columns, axis=0, keepdims=True) * (1.0 / depth)
-    columns = columns - jnp.where(here == 0, mean, 0.0)
-    columns = table_times(ztab.at[0:2], columns) * kern[...]
-    columns = table_times(ztab.at[2:4], columns)
+    mean = jnp.where(here == 0, jnp.sum(columns, axis=0, keepdims=True) * (1.0 / depth), 0.0)
+    number = lax.rem(lax.broadcasted_iota(jnp.int32, (came, per * lanes), 0), 2 * (planes + 2))
+    count = len(inside)
+    number = number - 2 * count
+    number = jnp.where(number >= len(outside), number - len(outside), number)
+    columns = jnp.where((number == 0) | (number == 1), columns, columns - mean)
+    columns = table_times((ztab[0, :, :came], ztab[1, :, :came]), columns) * kern[...]
+    columns = table_times((ztab[2, :, :depth], ztab[3, :, :depth]), columns)
     for row in range(per):
         rout[pl.ds(row, depth, stride=per), :] = columns[:, row * lanes : (row + 1) * lanes]
 
@@ -579,7 +585,7 @@
         hop_two(plane).wait_send()
         hop_pass(plane).wait_send()
 
-    loop(1, planes + 1, drain)
+    loop(0, planes + 2, drain)
     for piece_number in range(2):
         for side in range(2):
             in_sent(piece_number, side)
@@ -593,38 +599,36 @@
         to_across(part).wait_recv()
         pass_on(part).start()
 
-    def share(part):
-        slot = pl.ds(4 * core + 2 * part, 2)
-        return remote(pot.at[slot], pot.at[slot], (e_s, e_r), part, sibling)
+    def share(part, pair):
+        slot = 4 * core + 2 * part + pair
+        return remote(pot.at[slot], pot.at[slot], (e_s, e_r), 2 * part + pair, sibling)
 
     def invert(part):
         to_partner(part).wait_recv()
         pass_on(part).wait_recv()
-        columns = []
-        for plane in range(planes // 2):
-            blocks = [
-                quads[which, part, pl.ds(plane * per + row, layer, stride=piece), :]
-                for which in range(4)
-                for row in range(per)
+        for pair in range(2):
+            columns = []
+            for plane in (2 * pair, 2 * pair + 1):
+                blocks = [
+                    quads[which, part, pl.ds(plane * per + row, layer, stride=piece), :]
+                    for which in range(4)
+                    for row in range(per)
+                ]
+                columns.append(jnp.concatenate(blocks, axis=0))
+            pot[4 * core + 2 * part + pair] = table_times(tab.at[0:2], jnp.concatenate(columns, axis=1))
+            share(part, pair).start()
+
+    def finish(part):
+        for pair in range(2):
+            share(part, pair).wait_recv()
+            sides = [pot[4 * side + 2 * part + pair] for side in range(2)]
+            value = [
+                jnp.concatenate([side[:, plane * lanes : (plane + 1) * lanes] for side in sides], axis=1)
+                for plane in range(2)
             ]
-            columns.append(jnp.concatenate(blocks, axis=0))
-        value = table_times(tab.at[0:2], jnp.concatenate(columns, axis=1))
-        for pair in range(2):
-            pot[4 * core + 2 * part + pair] = value[:, pair * cols : (pair + 1) * cols]
-        share(part).start()
-
-    def finish(part):
-        share(part).wait_recv()
-        value = [
-            jnp.concatenate(
-                [pot[4 * side + 2 * part + plane // 2, :, plane % 2 * lanes : (plane % 2 + 1) * lanes] for side in range(2)],
-                axis=1,
-            )
-            for plane in range(planes // 2)
-        ]
-        value = times_table(jnp.concatenate(value, axis=0), tab.at[0:2])
-        for plane in range(planes // 2):
-            out_ref[part * (planes // 2) + plane] = value[plane * rows : (plane + 1) * rows]
+            value = times_table(jnp.concatenate(value, axis=0), tab.at[0:2])
+            for plane in range(2):
+                out_ref[part * (planes // 2) + 2 * pair + plane] = value[plane * rows : (plane + 1) * rows]
 
     invert(0)
     finish(0)
@@ -635,7 +639,8 @@
         to_partner(part).wait_send()
         to_across(part).wait_send()
         pass_on(part).wait_send()
-        share(part).wait_send()
+        for pair in range(2):
+            share(part, pair).wait_send()
 
 
 def per_device(probes, potential, potential_change, coefficients):
@@ -643,6 +648,7 @@
     slabs = lax.axis_size("slab")
     layer = slabs // 2
     depth = planes * slabs
+    half = rows // 2
     fourth = rows // 4
     size = 2 * planes * (fourth // layer)
     vmem = pl.BlockSpec(memory_space=pltpu.VMEM)
@@ -654,10 +660,17 @@
     high, low = cas_split(depth)
     spots = np.arange(layer)[:, None, None, None] // 4 * 8 + np.arange(layer)[:, None, None, None] % 4
     halves = np.arange(2)[None, None, :, None] * 4
-    inner = np.array([list(range(2, planes - 2)), [0, 1, planes - 2, planes - 1]])[None, :, None, :]
-    came = ((spots + halves) * planes + inner).reshape(-1)
+    inner = [list(range(2, planes - 2)), [-1, planes, 0, 1, planes - 2, planes - 1]]
+    came = [
+        (np.arange(layer)[:, None, None] // 4 * 8 + np.arange(layer)[:, None, None] % 4 + halves[0, 0]) * planes
+        + np.array(group)
+        for group in inner
+    ]
+    came = np.concatenate([part.reshape(layer, -1) for part in came], axis=1).reshape(-1) % depth
     goes = ((spots[:, 0] + halves[:, 0]) * planes + np.arange(planes)).reshape(-1)
-    deep = tables((high[:, came], low[:, came]), (high[goes], low[goes]))
+    extra = np.zeros((depth, len(came) - depth), high.dtype)
+    back = [np.concatenate([part[goes], extra], axis=1) for part in (high, low)]
+    deep = tables((high[:, came], low[:, came]), back)
     tall = rows + 2 * PAD
     hartree_change, total = pl.pallas_call(
         functools.partial(response_kernel, slabs, layer),
@@ -672,23 +685,23 @@
             pltpu.VMEM((panel, planes + 2, rows, cols), BF16),
             pltpu.VMEM((planes, rows, cols), F32),
             pltpu.VMEM((planes, rows, cols), F32),
-            pltpu.VMEM((4, rows, cols), F32),
+            pltpu.VMEM((2, rows, cols), F32),
+            pltpu.VMEM((2, half, cols), BF16),
+            pltpu.VMEM((2, rows, cols), BF16),
             pltpu.VMEM((planes + 2, 2, rows, 128), F32),
             pltpu.VMEM((planes + 2, 2, rows, 128), F32),
             pltpu.VMEM((panel, planes + 2, 2, tall, 128), F32),
             pltpu.VMEM((panel, planes + 2, 2, tall, 128), F32),
             pltpu.VMEM((panel, planes + 2, 2, tall, 128), F32),
             pltpu.VMEM((panel, planes + 2, 2, tall, 128), F32),
-            pltpu.VMEM((planes + 1, rows, cols), F32),
-            pltpu.VMEM((2, rows, cols), BF16),
-            pltpu.VMEM((2, rows, cols), BF16),
-            pltpu.VMEM((planes + 1, 2, rows, 128), F32),
-            pltpu.VMEM((planes + 1, rows, 128), F32),
-            pltpu.VMEM((planes + 1, 2, fourth, 128), F32),
+            pltpu.VMEM((planes + 2, rows, cols), F32),
+            pltpu.VMEM((planes + 2, 2, rows, 128), F32),
+            pltpu.VMEM((planes + 2, rows, 128), F32),
+            pltpu.VMEM((planes + 2, 2, fourth, 128), F32),
             pltpu.VMEM((7, 24, cols), F32),
-            pltpu.VMEM((4, depth, depth), BF16),
-            pltpu.VMEM((2, layer * size // 2, 128), F32),
-            pltpu.VMEM((layer * size, 128), F32),
+            pltpu.VMEM((4, depth, len(came)), BF16),
+            pltpu.VMEM((2, len(came) // 2 * 4, 128), F32),
+            pltpu.VMEM((len(came) * 4, 128), F32),
             pltpu.VMEM((depth, 4 * 128), F32),
             pltpu.VMEM((layer * size, 128), F32),
             pltpu.VMEM((2, layer * size // 4, 128), F32),
@@ -697,16 +710,15 @@
             dma((5,)),
             dma((6,)), dma((6,)),
             dma((4,)), dma((4,)),
-            dma((2,)), dma((2,)),
-            dma((planes + 1,)), dma((planes + 1,)),
-            dma((2, planes + 1)), dma((2, planes + 1)),
+            dma((planes + 2,)), dma((planes + 2,)),
+            dma((2, planes + 2)), dma((2, planes + 2)),
             dma((3,)), dma((3,)),
             dma((2, 2, layer)), dma((2, 2, layer)),
             dma((2, 2, layer)), dma((2, 2, layer)),
             dma((2,)), dma((2,)),
             dma((2,)), dma((2,)),
             dma((2,)), dma((2,)),
-            dma((2,)), dma((2,)),
+            dma((4,)), dma((4,)),
             dma((2, 4)), dma((2, 4)),
             pltpu.SemaphoreType.REGULAR((2,)),
         ],

time: 80.3 us -> 77.5 us (0.965)
  Pallas kernels: 77.6 us -> 74.8 us
    pallas_call x1, Pallas kernels: 77.6 us -> 74.8 us  [per_device(): pl.pallas_call(functools.partial(response_kernel, slabs, layer), out_shap...]
where the time goes in v6:
time: 77.5 us; the launch traced here: 77.4 us
  Pallas kernels  74.8 us (97%)
  local copies, waits for them, and re-layouts  1.33 us (2%)
    pallas_call x1, Pallas kernels, per_device(): pl.pallas_call(functools.partial(response_kernel, slabs, layer), out_shap...  74.8 us

profile of v6, /device:TPU:1, one launch (start us, length us, event | category | flops | bytes accessed | tf_op | source)
XLA Modules:
  0.0 77.4 jit_solution(9843851472378565918)
XLA Ops:
  0.6 74.8 %response.1 = (f32[8,256,256]{2,1,0:T(8,128)S(1)}, f32[8,128]{1,0:T(8,128)}) custom-call(f32[3]{0:T(128)} %coef_ref.1, bf16[4,256,256]{2,1,0:T(8,128)(2,1)} %constant.9.clone.table_ref, bf16[4,256,320]{2,1,0:T(8,128)(2,1)} %constant.10.clone.ztable_ref, bf16[2,8,256,256]{3,2,1,0:T(8,128)(2,1)} %probes_ref.1, f32[8,256,256]{2,1,0:T(8,128)} %pot_ref.1, ...), custom_call_target="tpu_custom_call" | custom-call | tf_op jit(solution)/shard_map/response/pallas_call | solution.py:675
  75.4 0.0 copy-start
  75.4 0.0 copy-start.1
  75.4 1.3 %copy.10 = f32[8,256,256]{2,1,0:T(8,128)} copy(f32[8,256,256]{2,1,0:T(8,128)S(1)} %get-tuple-element.6) | data formatting | bytes 4194304
  76.8 0.0 copy-done
  76.8 0.0 copy-done.1
  76.8 0.6 multiply_reduce_fusion
Async XLA Ops:
  75.4 1.3 %copy-start = (f32[3,1]{1,0:T(4,128)S(1)}, f32[3,1]{1,0:T(4,128)}, u32[]{:S(2)}) copy-start(f32[3,1]{1,0:T(4,128)} %constant.16) | copy-start | bytes 40
  75.4 1.3 %copy-start.1 = (f32[8,128]{1,0:T(8,128)S(1)}, f32[8,128]{1,0:T(8,128)}, u32[]{:S(2)}) copy-start(f32[8,128]{1,0:T(8,128)} %get-tuple-element.5) | copy-start | bytes 12292

commit v7 on v6

--- a/solution.py
+++ b/solution.py
@@ -428,20 +428,20 @@
     both(merge, 0, planes + 1)
     both(last, 2, planes - 1)
     transform([2, planes - 1])
-    for plane in inside:
-        relay(plane)
-    pl.semaphore_wait(ready.at[1], 1)
-    in_start(0, 1)
     both(merge, 2, planes - 1)
-    for plane in inside:
-        settle(plane)
-    in_start(0, 0)
     level(0, 0)
     level(planes + 1, 1)
     first(0, (1,))
     first(planes + 1, (-1,))
     both(last, 1, planes)
     transform([1, planes])
+    for plane in inside:
+        relay(plane)
+    pl.semaphore_wait(ready.at[1], 1)
+    in_start(0, 1)
+    for plane in inside:
+        settle(plane)
+    in_start(0, 0)
 
     mom = (mom_s, mom_r)
     for order in range(3):

time: 77.5 us -> 77.3 us (level)
  no operation moved by 1% of the time
where the time goes in v7:
time: 77.3 us; the launch traced here: 77.2 us
  Pallas kernels  74.6 us (97%)
  local copies, waits for them, and re-layouts  1.33 us (2%)
    pallas_call x1, Pallas kernels, per_device(): pl.pallas_call(functools.partial(response_kernel, slabs, layer), out_shap...  74.6 us

profile of v7, /device:TPU:1, one launch (start us, length us, event | category | flops | bytes accessed | tf_op | source)
XLA Modules:
  0.0 77.2 jit_solution(2678418528868315803)
XLA Ops:
  0.6 74.6 %response.1 = (f32[8,256,256]{2,1,0:T(8,128)S(1)}, f32[8,128]{1,0:T(8,128)}) custom-call(f32[3]{0:T(128)} %coef_ref.1, bf16[4,256,256]{2,1,0:T(8,128)(2,1)} %constant.9.clone.table_ref, bf16[4,256,320]{2,1,0:T(8,128)(2,1)} %constant.10.clone.ztable_ref, bf16[2,8,256,256]{3,2,1,0:T(8,128)(2,1)} %probes_ref.1, f32[8,256,256]{2,1,0:T(8,128)} %pot_ref.1, ...), custom_call_target="tpu_custom_call" | custom-call | tf_op jit(solution)/shard_map/response/pallas_call | solution.py:675
  75.2 0.0 copy-start
  75.2 0.0 copy-start.1
  75.2 1.3 %copy.10 = f32[8,256,256]{2,1,0:T(8,128)} copy(f32[8,256,256]{2,1,0:T(8,128)S(1)} %get-tuple-element.6) | data formatting | bytes 4194304
  76.6 0.0 copy-done
  76.6 0.0 copy-done.1
  76.6 0.6 multiply_reduce_fusion
Async XLA Ops:
  75.2 1.3 %copy-start = (f32[3,1]{1,0:T(4,128)S(1)}, f32[3,1]{1,0:T(4,128)}, u32[]{:S(2)}) copy-start(f32[3,1]{1,0:T(4,128)} %constant.16) | copy-start | bytes 40
  75.2 1.3 %copy-start.1 = (f32[8,128]{1,0:T(8,128)S(1)}, f32[8,128]{1,0:T(8,128)}, u32[]{:S(2)}) copy-start(f32[8,128]{1,0:T(8,128)} %get-tuple-element.5) | copy-start | bytes 12292
